TPU v7x, 128 devices: a whole 4x4x4 slice. The times are simulated.
128 devices in a mesh: frame: 2 (over y_hi), plane: 64 (over z, y_lo, x, core).
Axes of the slice: x: 4, y: 4 (y_hi: 2, y_lo: 2; y = y_hi * 2 + y_lo), z: 4, core: 2. Of those that a mesh axis runs over, the one named last changes fastest.
Arguments:
- states: float32 [4, 2, 64, 256, 256], P(None, 'frame', 'plane'), may hold values from -6 to 6
- measured: float32 [2, 64, 256, 256], P('frame', 'plane'), may hold values from -6 to 6
- response: float32 [256, 256], replicated, may hold values from 0.1 to 10
- kernel_in: bfloat16 [3, 9, 32, 2], replicated, may hold values from -1.5 to 1.5
- bias_in: float32 [3, 32], replicated, may hold values from -3 to 3
- kernel_mid: bfloat16 [3, 1, 9, 32, 32], replicated, may hold values from -0.375 to 0.375
- bias_mid: float32 [3, 1, 32], replicated, may hold values from -3 to 3
- kernel_out: bfloat16 [3, 9, 32], replicated, may hold values from -0.375 to 0.375
Outputs:
- new_states: float32 [4, 2, 64, 256, 256], P(None, 'frame', 'plane')
All inputs are finite; a program needn't handle non-finite values.
Results may differ from a plain program's by a relative error of at most 0.0056.
Values may be sent and summed in bfloat16 or wider, within the bound.
A program may use at most 192 MiB of HBM per device.

v0:
```python
import functools
import math

import jax
import jax.numpy as jnp
import numpy as np
from jax import lax
from jax.experimental import pallas as pl
from jax.experimental.pallas import tpu as pltpu
from jax.sharding import PartitionSpec as P

relaxation = 0.8

GROUPS = [(0, 0), (0, 1), (3, 0), (3, 1), (1, 0), (1, 1), (2, 0), (2, 1)]
STRIP = 16


def block_order(width):
    blocks = width // 2
    per = blocks // STRIP
    lane = np.arange(blocks)
    return (lane % STRIP) * per + lane // STRIP


def spread_table(width):
    blocks = width // 2
    order = block_order(width)
    table = np.zeros((width, 4 * blocks), np.float32)
    for xo in range(4):
        for lane in range(blocks):
            col = 2 * order[lane] + xo - 1
            if 0 <= col < width:
                table[col, xo * blocks + lane] = 1
    return table


def gather_table(width):
    blocks = width // 2
    order = block_order(width)
    table = np.zeros((width, width), np.float32)
    for j in range(2):
        for lane in range(blocks):
            table[j * blocks + lane, 2 * order[lane] + j] = 1
    return table


def select_in():
    chosen = np.zeros((9, 4, 24, 2, 8), np.float32)
    for half in range(2):
        for g, (i, j) in enumerate(GROUPS):
            for p in range(3):
                for q in range(3):
                    chosen[3 * p + q, j + q, 7 + 4 * half + i + p, half, g] = 1
    return chosen.reshape(9, 96, 16)


def slots_mid():
    slots = list(GROUPS)
    slots += [(i, -1 if j == 1 else 2) for i, j in GROUPS]
    slots += [(-1 if i == 3 else 4, j) for i, j in GROUPS[:4]]
    slots += [(-1 if i == 3 else 4, -1 if j == 1 else 2) for i, j in GROUPS[:4]]
    return slots


def select_mid():
    chosen = np.zeros((9, 24, 8), np.float32)
    for s, (row, col) in enumerate(slots_mid()):
        for g, (i, j) in enumerate(GROUPS):
            p, q = row - i + 1, col - j + 1
            if 0 <= p < 3 and 0 <= q < 3:
                chosen[3 * p + q, s, g] = 1
    return chosen


def select_out():
    targets = [None] * 32
    for j in range(2):
        far = 2 if j == 0 else -1
        for i in range(4):
            targets[j * 4 + i] = (i, j)
            targets[8 + j * 4 + i] = (i, far)
        for base, col in ((16, j), (24, far)):
            targets[base + j * 4] = (4, col)
            targets[base + j * 4 + 3] = (-1, col)
    chosen = np.zeros((9, 32, 8), np.float32)
    for r, target in enumerate(targets):
        if target is None:
            continue
        for g, (i, j) in enumerate(GROUPS):
            p, q = i - target[0] + 1, j - target[1] + 1
            if 0 <= p < 3 and 0 <= q < 3:
                chosen[3 * p + q, r, g] = 1
    return chosen


def banded(kernel_in, bias_in, kernel_mid, bias_mid, kernel_out):
    kind = jnp.bfloat16
    d, _, channels, _ = kernel_in.shape
    first = jnp.einsum("tsg,dtoc->dcsgo", select_in().astype(kind), kernel_in, preferred_element_type=kind)
    first = first.reshape(d, 192, 16 * channels)
    mid = jnp.einsum("tsg,dtoc->dscgo", select_mid().astype(kind), kernel_mid[:, 0], preferred_element_type=kind)
    mid = mid.reshape(d, 24 * channels, 8 * channels)
    last = jnp.einsum("trg,dtc->drgc", select_out().astype(kind), kernel_out, preferred_element_type=kind)
    last = last.reshape(d, 32, 8 * channels)
    bias_first = jnp.tile(bias_in[:, None], (1, 1, 16))
    bias_second = jnp.tile(bias_mid[:, 0][:, None], (1, 1, 8))
    return first, bias_first, mid, bias_second, last


def mm(a, b, dims=((1,), (0,))):
    return lax.dot_general(a, b, (dims, ((), ())), preferred_element_type=jnp.float32)


def denoise(x, w_first, b_first, w_mid, b_mid, w_last, spread, gather, emit, u_ref, h_ref, c_ref, d_ref, frames):
    rows = u_ref.shape[1] - 16
    row_blocks = rows // 4
    kind = jnp.bfloat16
    for pair in range(len(x)):
        for ch in range(2):
            u_ref[pair * 2 + ch, :8, :] = jnp.zeros((8, 512), jnp.float32)
            u_ref[pair * 2 + ch, rows + 8:, :] = jnp.zeros((8, 512), jnp.float32)
            u_ref[pair * 2 + ch, 8:rows + 8, :] = mm(x[pair][ch](), spread)
    for img in range(len(x) * frames):
        h_ref[img, 0] = jnp.zeros((160, 256), kind)
        h_ref[img, row_blocks + 1] = jnp.zeros((160, 256), kind)

    first_row = lax.broadcasted_iota(jnp.int32, (16, 256), 0) == 0
    last_row = lax.broadcasted_iota(jnp.int32, (16, 256), 0) == 15

    def first_layer(k, carry):
        start = pl.multiple_of(k * 8, 8)
        for pair in range(len(x)):
            parts = [
                u_ref[pair * 2 + ch, pl.ds(start, 24), xo * 128:(xo + 1) * 128]
                for ch in range(2) for xo in range(4)
            ]
            for f in range(frames):
                ordered = parts if f == 0 else parts[4:] + parts[:4]
                stacked = jnp.concatenate(ordered, 0).astype(kind)
                made = mm(stacked, w_first[...], ((0,), (0,)))
                made = jnp.maximum(made + b_first[...], 0.0)
                for half in range(2):
                    piece = made[:, half * 256:(half + 1) * 256]
                    at = 2 * k + half + 1
                    img = pair * frames + f
                    h_ref[img, at, 16:144, :] = piece.astype(kind)
                    h_ref[img, at, 0:16, :] = jnp.where(first_row, 0.0, pltpu.roll(piece[112:128], 1, 0)).astype(kind)
                    h_ref[img, at, 144:160, :] = jnp.where(last_row, 0.0, pltpu.roll(piece[0:16], 15, 0)).astype(kind)
        return carry

    lax.fori_loop(0, rows // 8, first_layer, 0)

    right = (lax.broadcasted_iota(jnp.int32, (128, 256), 1) // 32) % 2 == 1
    right_half = right[:, :128]
    low = lax.broadcasted_iota(jnp.int32, (128, 128), 1) >= 64

    for img in range(len(x) * frames):

        def mid_layer(a, carry):
            here = h_ref[img, a + 1, 16:144, :]
            side = jnp.where(right, h_ref[img, a + 1, 0:128, :], h_ref[img, a + 1, 32:160, :])
            across = jnp.where(low, h_ref[img, a, 16:144, 0:128], h_ref[img, a + 2, 16:144, 0:128])
            corner_left = jnp.where(low, h_ref[img, a, 0:128, 0:128], h_ref[img, a + 2, 0:128, 0:128])
            corner_right = jnp.where(low, h_ref[img, a, 32:160, 0:128], h_ref[img, a + 2, 32:160, 0:128])
            corner = jnp.where(right_half, corner_left, corner_right)
            made = mm(jnp.concatenate([here, side, across, corner], 1), w_mid[...])
            hidden = jnp.maximum(made + b_mid[...], 0.0).astype(kind)
            c_ref[img, a + 1] = mm(w_last[...], hidden, ((1,), (1,)))
            return carry

        lax.fori_loop(0, row_blocks, mid_layer, 0, unroll=2)

    lane = lax.broadcasted_iota(jnp.int32, (8, 128), 1)
    sub = lax.broadcasted_iota(jnp.int32, (8, 128), 0)

    def moved(value):
        before = jnp.where(lane >= 16, pltpu.roll(value, 16, 1), jnp.where(lane >= 1, pltpu.roll(value, 17, 1), 0.0))
        after = jnp.where(lane < 112, pltpu.roll(value, 112, 1), jnp.where(lane < 127, pltpu.roll(value, 111, 1), 0.0))
        return jnp.where(sub < 4, before, after)

    for img in range(len(x) * frames):
        c_ref[img, 0] = jnp.zeros((32, 128), jnp.float32)
        c_ref[img, row_blocks + 1] = jnp.zeros((32, 128), jnp.float32)

        def column_sums(a, carry):
            c_ref[img, a, 0:8, :] += moved(c_ref[img, a, 8:16, :])
            c_ref[img, a, 16:24, :] += moved(c_ref[img, a, 24:32, :])
            return carry

        lax.fori_loop(1, row_blocks + 1, column_sums, 0, unroll=4)

        def row_sums(k, carry):
            blocks = []
            for half in range(2):
                a = 2 * k + half + 1
                value = c_ref[img, a, 0:8, :]
                value += jnp.where(sub % 4 == 0, c_ref[img, a - 1, 16:24, :], 0.0)
                value += jnp.where(sub % 4 == 3, c_ref[img, a + 1, 16:24, :], 0.0)
                blocks.append(value)
            start = pl.multiple_of(k * 8, 8)
            d_ref[img, pl.ds(start, 8), 0:128] = jnp.where(sub < 4, blocks[0], pltpu.roll(blocks[1], 4, 0))
            d_ref[img, pl.ds(start, 8), 128:256] = jnp.where(sub < 4, pltpu.roll(blocks[0], 4, 0), blocks[1])
            return carry

        lax.fori_loop(0, rows // 8, row_sums, 0, unroll=4)
        emit(img // frames, img % frames, mm(d_ref[img].astype(kind), gather))


def scratch(pairs, frames, rows):
    images = pairs * frames
    return [
        pltpu.VMEM((pairs * 2, rows + 16, 512), jnp.float32),
        pltpu.VMEM((images, rows // 4 + 2, 160, 256), jnp.bfloat16),
        pltpu.VMEM((images, rows // 4 + 2, 32, 128), jnp.float32),
        pltpu.VMEM((images, rows, 256), jnp.float32),
    ]


def z_kernel(measured, states, response, own, other, cosine, sines, w_first, b_first, w_mid, b_mid, w_last, spread, gather, data_out, res_out, *scratches):
    kind = jnp.bfloat16
    cos, sin = cosine[...], sines[...]
    source = (measured[...] + states[0]).astype(kind)
    row_real = mm(source, cos).astype(kind)
    row_imag = (-mm(source, sin)).astype(kind)
    gain = 1.0 / (1.0 + response[...])
    spec_real = ((mm(cos, row_real) + mm(sin, row_imag)) * gain).astype(kind)
    spec_imag = ((mm(cos, row_imag) - mm(sin, row_real)) * gain).astype(kind)
    back_real = (mm(cos, spec_real) - mm(sin, spec_imag)).astype(kind)
    back_imag = (mm(cos, spec_imag) + mm(sin, spec_real)).astype(kind)
    data_out[...] = (mm(back_real, cos) - mm(back_imag, sin)) * (1.0 / (source.shape[0] * source.shape[1]))

    def emit(pair, f, value):
        res_out[...] = value.astype(kind)

    denoise([(lambda: own[...], lambda: other[...])], w_first.at[0], b_first.at[0], w_mid.at[0], b_mid.at[0], w_last.at[0], spread[...], gather[...], emit, *scratches, frames=1)


def xy_kernel(planes, w_first, b_first, w_mid, b_mid, w_last, spread, gather, res_out, *scratches):
    for which in range(2):

        def emit(pair, f, value):
            res_out[which, pair, f] = value.astype(jnp.bfloat16)

        pairs = [(lambda p=p: planes[which, p, 0], lambda p=p: planes[which, p, 1]) for p in range(2)]
        d = which + 1
        denoise(pairs, w_first.at[d], b_first.at[d], w_mid.at[d], b_mid.at[d], w_last.at[d], spread[...], gather[...], emit, *scratches, frames=2)


def final_kernel(states, data, res_z, back_x, back_y, out):
    w = [states[k] for k in range(4)]
    res_x = jnp.transpose(back_x[...].astype(jnp.float32))
    z = [
        2.0 * data[...] - w[0],
        w[1] - 2.0 * res_z[...].astype(jnp.float32),
        w[2] - 2.0 * res_x,
        w[3] - 2.0 * back_y[...].astype(jnp.float32),
    ]
    twice = 0.5 * (z[0] + z[1] + z[2] + z[3])
    for k in range(4):
        out[k] = (1.0 - relaxation) * w[k] + relaxation * (twice - z[k])


VM = pl.BlockSpec(memory_space=pltpu.VMEM)


def call(kernel, out_shape, args, scratch_shapes, flops):
    return pl.pallas_call(
        kernel,
        out_shape=out_shape,
        in_specs=[VM] * len(args),
        out_specs=jax.tree.map(lambda _: VM, out_shape),
        scratch_shapes=scratch_shapes,
        compiler_params=pltpu.CompilerParams(vmem_limit_bytes=56 * 2**20),
        cost_estimate=pl.CostEstimate(flops=flops, bytes_accessed=2**21, transcendentals=0),
    )(*args)


def fourier_tables(length):
    indices = jnp.arange(length, dtype=jnp.int32)
    phase = indices[:, None] * indices[None, :] % length
    angle = phase.astype(jnp.float32) * (2.0 * math.pi / length)
    return (jnp.cos(angle).astype(jnp.bfloat16), jnp.sin(angle).astype(jnp.bfloat16))


def on_device(states, measured, response, kernel_in, bias_in, kernel_mid, bias_mid, kernel_out):
    kind = jnp.bfloat16
    current = states[:, 0, 0]
    width = current.shape[-1]
    rounded = current[1:].astype(kind)
    devices = lax.axis_size("frame") * lax.axis_size("plane")
    depth = lax.axis_size("plane")
    partner = lax.ppermute(rounded[0], "frame", [(0, 1), (1, 0)])
    leaving = jnp.stack([jnp.transpose(rounded[1]), rounded[2]])
    leaving = leaving.reshape(2, devices, width // devices, width).transpose(1, 0, 2, 3)
    arrived = lax.all_to_all(leaving, ("frame", "plane"), split_axis=0, concat_axis=0, tiled=True)
    planes = arrived.reshape(2, depth, 2, width // devices, width).transpose(2, 3, 0, 1, 4)
    weights = banded(kernel_in, bias_in, kernel_mid, bias_mid, kernel_out)
    cosine, sines = fourier_tables(width)
    spread = jnp.asarray(spread_table(width), kind)
    gather = jnp.asarray(gather_table(width), kind)
    image = jax.ShapeDtypeStruct((width, width), kind)
    data, res_z = call(
        z_kernel,
        (jax.ShapeDtypeStruct((width, width), jnp.float32), image),
        (measured[0, 0], current, response, rounded[0], partner, cosine, sines) + weights + (spread, gather),
        scratch(1, 1, width),
        4 * 10**9,
    )
    residuals = call(
        xy_kernel,
        jax.ShapeDtypeStruct((2, 2, 2, depth, width), kind),
        (planes,) + weights + (spread, gather),
        scratch(2, 2, depth),
        8 * 10**9,
    )
    returning = residuals.transpose(2, 3, 0, 1, 4).reshape(devices, 2, width // devices, width)
    returned = lax.all_to_all(returning, ("frame", "plane"), split_axis=0, concat_axis=0, tiled=True)
    returned = returned.transpose(1, 0, 2, 3).reshape(2, width, width)
    out = call(
        final_kernel,
        jax.ShapeDtypeStruct(current.shape, jnp.float32),
        (current, data, res_z, returned[0], returned[1]),
        [],
        10**6,
    )
    return out[:, None, None]


def solution(mesh):
    placed = (
        P(None, "frame", "plane", None, None),
        P("frame", "plane", None, None),
        P(),
        P(),
        P(),
        P(),
        P(),
        P(),
    )
    return jax.shard_map(
        on_device,
        mesh=mesh,
        in_specs=placed,
        out_specs=P(None, "frame", "plane", None, None),
        check_vma=False,
    )
```

profile of v0, /device:TPU:1, one launch (start us, length us, event | category | flops | bytes accessed | tf_op | source)
XLA Modules:
  0.0 145.6 jit_solution(14508812444880335102)
XLA Ops:
  0.0 1.3 convert.3
  1.4 0.0 copy-start.1
  1.4 3.8 %collective-permute-start = (bf16[256,256]{1,0:T(8,128)(2,1)S(1)}, bf16[256,256]{1,0:T(8,128)(2,1)S(1)}, u32[]{:S(2)}, u32[]{:S(2)}) collective-permute-start(bf16[256,256]{1,0:T(8,128)(2,1)S(1)} %get-tuple-element.11.own), channel_id=1, source_target_pairs={{0,64},{64,0},{1,65},{65,1},{2,66},{66,2},{3,67},{67,3},{4,68},{68... | collective-permute-start | bytes 393224 | tf_op jit(solution)/shard_map/ppermute | solution.py:292
  5.2 0.1 copy.43
  5.3 0.1 stack.8
  5.4 0.1 stack.9
  5.4 0.4 maximum_bitcast_fusion
  5.8 0.9 copy.44
  6.7 8.8 %all-to-all-start = ((bf16[128,2,2,256]{3,2,1,0:T(2,128)(2,1)}), bf16[128,2,2,256]{3,2,1,0:T(2,128)(2,1)S(1)}, u32[]{:S(2)}, u32[]{:S(2)}) async-start(bf16[128,2,2,256]{3,2,1,0:T(2,128)(2,1)} %copy.44), calls=%async_computation | async-start | bytes 524288 | tf_op jit(solution)/shard_map/all_to_all | solution.py:295
  15.5 0.0 copy-done.4
  15.5 0.0 copy-done
  15.5 3.1 %convolution_bitcast_fusion = bf16[3,24,32,8,32]{2,1,4,0,3:T(8,128)(2,1)} fusion(bf16[9,24,8,1,1]{1,0,4,3,2:T(8,128)(2,1)S(1)} %copy-done.4, bf16[3,9,32,32]{3,2,1,0:T(8,128)(2,1)S(1)} %bitcast.66), kind=kOutput, calls=%fused_computation | convolution fusion | flops 10616832 | bytes 1238400 | tf_op jit(solution)/shard_map/tsg,dtoc->dscgo/dot_general | solution.py:101
  18.7 9.3 %copy.39 = bf16[3,24,32,8,32]{4,3,2,1,0:T(8,128)(2,1)} copy(bf16[3,24,32,8,32]{2,1,4,0,3:T(8,128)(2,1)} %convolution_bitcast_fusion) | data formatting | bytes 2359296 | tf_op jit(solution)/shard_map/tsg,dtoc->dscgo/transpose | solution.py:101
  27.9 0.0 copy-done.1
  27.9 0.0 copy-start.5
  27.9 0.0 copy-start.6
  28.0 0.0 copy-start.7
  28.0 0.0 copy-start.8
  28.0 6.7 %reshape.45.w_mid = bf16[3,768,256]{2,1,0:T(8,128)(2,1)} reshape(bf16[3,24,32,8,32]{4,3,2,1,0:T(8,128)(2,1)} %copy.39) | data formatting | bytes 2359296 | tf_op jit(solution)/shard_map/reshape | solution.py:102
  34.6 0.0 copy-done.2
  34.6 0.0 copy-done.3
  34.6 0.4 convolution_bitcast_fusion.1
  35.0 0.8 copy.37
  35.8 0.5 reshape.44
  36.3 1.1 copy.42.w_first
  37.4 0.0 copy-done.5
  37.4 0.0 copy-done.6
  37.4 0.2 convolution_bitcast_fusion.2
  37.6 0.1 copy.41
  37.7 0.8 reshape.46.w_last
  38.5 0.0 copy-done.7
  38.5 0.7 tile.19.b_first
  39.2 0.0 copy-done.8
  39.2 0.7 tile.22.b_mid
  39.9 1.7 %sine_convert_fusion = (bf16[256,256]{1,0:T(8,128)(2,1)}, bf16[256,256]{1,0:T(8,128)(2,1)}) fusion(), kind=kLoop, calls=%fused_computation.12 | loop fusion | flops 1048576 | bytes 262144 | tf_op jit(solution)/shard_map/convert_element_type | solution.py:282
  41.6 0.0 all-to-all-done
  41.6 0.7 copy.45
  42.3 53.5 %shard_map.128 = bf16[2,2,2,64,256]{4,3,2,1,0:T(8,128)(2,1)} custom-call(bf16[2,2,2,64,256]{4,3,2,1,0:T(8,128)(2,1)} %bitcast.67, bf16[3,192,512]{2,1,0:T(8,128)(2,1)} %copy.42.w_first, f32[3,1,512]{2,1,0:T(1,128)} %tile.19.b_first, bf16[3,768,256]{2,1,0:T(8,128)(2,1)} %reshape.45.w_mid, f32[3,1,256]{2,1,0:T(1,128)} %tile.22.b_mid, ...), custom_call_target="tpu_custom_call" | custom-call | flops 8000000000 | bytes 2097152 | tf_op jit(solution)/shard_map/pallas_call | solution.py:267
  95.9 1.9 %copy.47 = bf16[128,2,2,256]{3,2,1,0:T(2,128)(2,1)} copy(bf16[128,2,2,256]{3,0,2,1:T(8,128)(2,1)} %bitcast.68) | data formatting | bytes 524288 | tf_op jit(solution)/shard_map/reshape | solution.py:316
  97.8 9.8 %all-to-all-start.1 = ((bf16[128,2,2,256]{3,2,1,0:T(2,128)(2,1)}), bf16[128,2,2,256]{3,2,1,0:T(2,128)(2,1)S(1)}, u32[]{:S(2)}, u32[]{:S(2)}) async-start(bf16[128,2,2,256]{3,2,1,0:T(2,128)(2,1)} %copy.47), calls=%async_computation.1 | async-start | bytes 524288 | tf_op jit(solution)/shard_map/all_to_all | solution.py:317
  107.5 0.0 collective-permute-done.other
  107.6 0.6 copy-done.9
  108.2 33.1 %shard_map.127 = (f32[256,256]{1,0:T(8,128)}, bf16[256,256]{1,0:T(8,128)(2,1)}) custom-call(f32[256,256]{1,0:T(8,128)} %bitcast.70, f32[4,256,256]{2,1,0:T(8,128)} %bitcast.63, f32[256,256]{1,0:T(8,128)} %response.1, bf16[256,256]{1,0:T(8,128)(2,1)} %copy-done.1, bf16[256,256]{1,0:T(8,128)(2,1)} %copy-done.9, bf16[256,256]{1,0:T(8,128)(2,1)} %get-tuple-element.15.cosine, ...), custom_call_target="tpu_custom_call" | custom-call | flops 4000000000 | bytes 2097152 | tf_op jit(solution)/shard_map/pallas_call | solution.py:267
  141.3 0.0 all-to-all-done.1
  141.4 0.2 fusion.12
  141.5 0.7 squeeze.27.back_x
  142.2 0.7 squeeze.28.back_y
  142.9 2.7 %shard_map.129 = f32[4,256,256]{2,1,0:T(8,128)} custom-call(f32[4,256,256]{2,1,0:T(8,128)} %bitcast.64, f32[256,256]{1,0:T(8,128)} %get-tuple-element.7.data, bf16[256,256]{1,0:T(8,128)(2,1)} %get-tuple-element.8.res_z, bf16[256,256]{1,0:T(8,128)(2,1)} %squeeze.27.back_x, bf16[256,256]{1,0:T(8,128)(2,1)} %squeeze.28.back_y), custom_call_target="tpu_custom_call" | custom-call | flops 1000000 | bytes 2097152 | tf_op jit(solution)/shard_map/pallas_call | solution.py:267
  (9 shorter events, 0.0 us)
Async XLA Ops:
  0.0 15.5 %copy-start.4 = (bf16[9,24,8,1,1]{1,0,4,3,2:T(8,128)(2,1)S(1)}, bf16[9,24,8,1,1]{1,0,4,3,2:T(8,128)(2,1)}, u32[]{:S(2)}) copy-start(bf16[9,24,8,1,1]{1,0,4,3,2:T(8,128)(2,1)} %constant.35) | copy-start | bytes 10372
  0.0 15.5 %copy-start = (bf16[3,1,9,32,32]{4,3,2,1,0:T(8,128)(2,1)S(1)}, bf16[3,1,9,32,32]{4,3,2,1,0:T(8,128)(2,1)}, u32[]{:S(2)}) copy-start(bf16[3,1,9,32,32]{4,3,2,1,0:T(8,128)(2,1)} %param.18) | copy-start | bytes 165892
  1.4 26.6 %copy-start.1 = (bf16[256,256]{1,0:T(8,128)(2,1)}, bf16[256,256]{1,0:T(8,128)(2,1)S(1)}, u32[]{:S(2)}) copy-start(bf16[256,256]{1,0:T(8,128)(2,1)S(1)} %get-tuple-element.11.own) | copy-start | bytes 393220
  1.4 106.2 %collective-permute-start = (bf16[256,256]{1,0:T(8,128)(2,1)S(1)}, bf16[256,256]{1,0:T(8,128)(2,1)S(1)}, u32[]{:S(2)}, u32[]{:S(2)}) collective-permute-start(bf16[256,256]{1,0:T(8,128)(2,1)S(1)} %get-tuple-element.11.own), channel_id=1, source_target_pairs={{0,64},{64,0},{1,65},{65,1},{2,66},{66,2},{3,67},{67,3},{4,68},{68... | collective-permute-start | bytes 393224 | tf_op jit(solution)/shard_map/ppermute | solution.py:292
  6.7 34.9 %all-to-all-start = ((bf16[128,2,2,256]{3,2,1,0:T(2,128)(2,1)}), bf16[128,2,2,256]{3,2,1,0:T(2,128)(2,1)S(1)}, u32[]{:S(2)}, u32[]{:S(2)}) async-start(bf16[128,2,2,256]{3,2,1,0:T(2,128)(2,1)} %copy.44), calls=%async_computation | async-start | bytes 524288 | tf_op jit(solution)/shard_map/all_to_all | solution.py:295
  27.9 6.7 %copy-start.2 = (bf16[9,96,16,1,1]{1,0,4,3,2:T(8,128)(2,1)S(1)}, bf16[9,96,16,1,1]{1,0,4,3,2:T(8,128)(2,1)}, u32[]{:S(2)}) copy-start(bf16[9,96,16,1,1]{1,0,4,3,2:T(8,128)(2,1)} %constant.34) | copy-start | bytes 82948
  27.9 6.7 %copy-start.3 = (bf16[3,9,32,2]{2,3,1,0:T(2,128)(2,1)S(1)}, bf16[3,9,32,2]{2,3,1,0:T(2,128)(2,1)}, u32[]{:S(2)}) copy-start(bf16[3,9,32,2]{2,3,1,0:T(2,128)(2,1)} %param.16) | copy-start | bytes 10372
  27.9 9.4 %copy-start.5 = (bf16[9,32,8,1]{1,0,3,2:T(8,128)(2,1)S(1)}, bf16[9,32,8,1]{1,0,3,2:T(8,128)(2,1)}, u32[]{:S(2)}) copy-start(bf16[9,32,8,1]{1,0,3,2:T(8,128)(2,1)} %constant.36) | copy-start | bytes 13828
  27.9 9.4 %copy-start.6 = (bf16[3,9,32]{2,0,1:T(4,128)(2,1)S(1)}, bf16[3,9,32]{2,0,1:T(4,128)(2,1)}, u32[]{:S(2)}) copy-start(bf16[3,9,32]{2,0,1:T(4,128)(2,1)} %param.20) | copy-start | bytes 5188
  28.0 10.5 %copy-start.7 = (f32[3,32]{1,0:T(4,128)S(1)}, f32[3,32]{1,0:T(4,128)}, u32[]{:S(2)}) copy-start(f32[3,32]{1,0:T(4,128)} %param.17) | copy-start | bytes 1156
  28.0 11.2 %copy-start.8 = (f32[3,1,32]{2,1,0:T(1,128)S(1)}, f32[3,1,32]{2,1,0:T(1,128)}, u32[]{:S(2)}) copy-start(f32[3,1,32]{2,1,0:T(1,128)} %param.19) | copy-start | bytes 1156
  97.8 43.6 %all-to-all-start.1 = ((bf16[128,2,2,256]{3,2,1,0:T(2,128)(2,1)}), bf16[128,2,2,256]{3,2,1,0:T(2,128)(2,1)S(1)}, u32[]{:S(2)}, u32[]{:S(2)}) async-start(bf16[128,2,2,256]{3,2,1,0:T(2,128)(2,1)} %copy.47), calls=%async_computation.1 | async-start | bytes 524288 | tf_op jit(solution)/shard_map/all_to_all | solution.py:317
  107.6 0.7 copy-start.9
where the time goes:
time: 146 us
  Pallas kernels  89.4 us (61%)
  local copies, waits for them, and re-layouts  26.5 us (18%)
  starting transfers between devices  22.4 us (15%)
  matrix products  3.77 us (3%)
  other arithmetic  3.42 us (2%)
    pallas_call x3, Pallas kernels, call(): pl.pallas_call(kernel, out_shape=out_shape, in_specs=[VM] * len(args), ou...  89.4 us
    all_to_all x1, starting transfers between devices, on_device(): lax.all_to_all(returning, ('frame', 'plane'), split_axis=0, concat_axis=0...  9.76 us
    transpose x1, local copies, waits for them, and re-layouts, banded(): jnp.einsum('tsg,dtoc->dscgo', select_mid().astype(kind), kernel_mid[:, 0]...  9.26 us
    all_to_all x1, starting transfers between devices, on_device(): lax.all_to_all(leaving, ('frame', 'plane'), split_axis=0, concat_axis=0,...  8.81 us
    reshape x1, local copies, waits for them, and re-layouts, banded(): mid = mid.reshape(d, 24 * channels, 8 * channels)  6.65 us
    ppermute x1, starting transfers between devices, on_device(): partner = lax.ppermute(rounded[0], 'frame', [(0, 1), (1, 0)])  3.82 us
    dot_general x1, matrix products, banded(): jnp.einsum('tsg,dtoc->dscgo', select_mid().astype(kind), kernel_mid[:, 0]...  3.14 us
  transfers between devices with their start and end apart: 3, of which 0 were waited for; matrix products, arithmetic and copies ran while one was open for 21% of the time, Pallas kernels for 60%

commit v1 on v0

v1 whole, which is shorter than its diff:
```python
import functools
import math

import jax
import jax.numpy as jnp
import numpy as np
from jax import lax
from jax.experimental import pallas as pl
from jax.experimental.pallas import tpu as pltpu
from jax.sharding import PartitionSpec as P

relaxation = 0.8

GROUPS = [(0, 0), (0, 1), (3, 0), (3, 1), (1, 0), (1, 1), (2, 0), (2, 1)]
STRIP = 16
FIRST_STEP = 8
MID_STEP = 16


def block_order(width):
    blocks = width // 2
    per = blocks // STRIP
    lane = np.arange(blocks)
    return (lane % STRIP) * per + lane // STRIP


def spread_table(width):
    blocks = width // 2
    order = block_order(width)
    table = np.zeros((width, 4 * blocks), np.float32)
    for xo in range(4):
        for lane in range(blocks):
            col = 2 * order[lane] + xo - 1
            if 0 <= col < width:
                table[col, xo * blocks + lane] = 1
    return table


def gather_table(width):
    blocks = width // 2
    order = block_order(width)
    table = np.zeros((width, width), np.float32)
    for j in range(2):
        for lane in range(blocks):
            table[j * blocks + lane, 2 * order[lane] + j] = 1
    return table


def select_in():
    chosen = np.zeros((9, 4, 24, 2, 8), np.float32)
    for half in range(2):
        for g, (i, j) in enumerate(GROUPS):
            for p in range(3):
                for q in range(3):
                    chosen[3 * p + q, j + q, 7 + 4 * half + i + p, half, g] = 1
    return chosen.reshape(9, 96, 16)


def slots_mid():
    slots = list(GROUPS)
    slots += [(i, -1 if j == 1 else 2) for i, j in GROUPS]
    slots += [(-1 if i == 3 else 4, j) for i, j in GROUPS[:4]]
    slots += [(-1 if i == 3 else 4, -1 if j == 1 else 2) for i, j in GROUPS[:4]]
    return slots


def select_mid():
    chosen = np.zeros((9, 24, 8), np.float32)
    for s, (row, col) in enumerate(slots_mid()):
        for g, (i, j) in enumerate(GROUPS):
            p, q = row - i + 1, col - j + 1
            if 0 <= p < 3 and 0 <= q < 3:
                chosen[3 * p + q, s, g] = 1
    return chosen


def select_out():
    targets = [None] * 32
    for j in range(2):
        far = 2 if j == 0 else -1
        for i in range(4):
            targets[j * 4 + i] = (i, j)
            targets[8 + j * 4 + i] = (i, far)
        for base, col in ((16, j), (24, far)):
            targets[base + j * 4] = (4, col)
            targets[base + j * 4 + 3] = (-1, col)
    chosen = np.zeros((9, 32, 8), np.float32)
    for r, target in enumerate(targets):
        if target is None:
            continue
        for g, (i, j) in enumerate(GROUPS):
            p, q = i - target[0] + 1, j - target[1] + 1
            if 0 <= p < 3 and 0 <= q < 3:
                chosen[3 * p + q, r, g] = 1
    return chosen


def first_table():
    chosen = select_in()
    table = np.zeros((2, 96, 16, 32), np.float32)
    for ch in range(2):
        for tap in range(9):
            table[ch, :, :, 2 * tap + ch] = chosen[tap]
    return table.reshape(192, 512)


def last_table():
    table = np.zeros((32, 8, 16), np.float32)
    table[:, :, :9] = select_out().transpose(1, 2, 0)
    return table.reshape(32, 128)


def mm(a, b, dims=((1,), (0,))):
    return lax.dot_general(a, b, (dims, ((), ())), preferred_element_type=jnp.float32)


def prepare(d, params, tables, built, frames):
    kernel_in, bias_in, kernel_mid, bias_mid, kernel_out = params
    first_at, last_at = tables
    w_first, b_first, w_mid, b_mid, w_last, spare = built
    kind = jnp.bfloat16
    lane = lax.broadcasted_iota(jnp.int32, (32, 512), 1)
    row = lax.broadcasted_iota(jnp.int32, (32, 512), 0)
    repeat = (lane % 32 == row).astype(jnp.float32)
    wide = repeat.astype(kind)
    narrow = wide[:, :256]

    spare[...] = jnp.zeros_like(spare)
    for tap in range(9):
        spare[2 * tap:2 * tap + 2, :] = mm(kernel_in[d, tap], wide, ((0,), (0,)))
    tiled = jnp.concatenate([spare[...]] * 16, 0)
    own = lax.broadcasted_iota(jnp.int32, (512, 512), 0) // 32 == lax.broadcasted_iota(jnp.int32, (512, 512), 1) // 32
    built_first = mm(first_at[...], jnp.where(own, tiled, 0.0).astype(kind)).astype(kind)
    w_first[:, 0:512] = built_first
    exact = lax.dot_general(bias_in[...], repeat, (((1,), (0,)), ((), ())), precision=lax.Precision.HIGHEST, preferred_element_type=jnp.float32)
    b_first[0:1, 0:512] = exact[d:d + 1]
    if frames == 2:
        w_first[0:96, 512:1024] = built_first[96:192]
        w_first[96:192, 512:1024] = built_first[0:96]
        b_first[0:1, 512:1024] = exact[d:d + 1]
    exact = lax.dot_general(bias_mid[:, 0, :], repeat[:, :256], (((1,), (0,)), ((), ())), precision=lax.Precision.HIGHEST, preferred_element_type=jnp.float32)
    b_mid[0:1, :] = exact[d:d + 1]

    taps = [mm(kernel_mid[d, 0, tap], narrow, ((0,), (0,))) for tap in range(9)]
    group = lane[:, :256] // 32
    for s, (r, c) in enumerate(slots_mid()):
        value = jnp.zeros((32, 256), jnp.float32)
        for g, (i, j) in enumerate(GROUPS):
            p, q = r - i + 1, c - j + 1
            if 0 <= p < 3 and 0 <= q < 3:
                value = jnp.where(group == g, taps[3 * p + q], value)
        w_mid[s * 32:(s + 1) * 32, :] = value.astype(kind)

    spare[9:16, 0:256] = jnp.zeros((7, 256), jnp.float32)
    spare[0:9, 0:256] = mm(kernel_out[d], narrow)
    tiled = jnp.concatenate([spare[0:16, 0:256]] * 8, 0)
    own = lax.broadcasted_iota(jnp.int32, (128, 256), 0) // 16 == lax.broadcasted_iota(jnp.int32, (128, 256), 1) // 32
    w_last[...] = mm(last_at[...], jnp.where(own, tiled, 0.0).astype(kind)).astype(kind)


def denoise(x, built, spread, gather, emit, u_ref, h_ref, c_ref, frames):
    w_first, b_first, w_mid, b_mid, w_last, _ = built
    rows = u_ref.shape[1] - 16
    row_blocks = rows // 4
    images = len(x) * frames
    kind = jnp.bfloat16
    for pair in range(len(x)):
        for ch in range(2):
            u_ref[pair * 2 + ch, :8, :] = jnp.zeros((8, 512), jnp.float32)
            u_ref[pair * 2 + ch, rows + 8:, :] = jnp.zeros((8, 512), jnp.float32)
            u_ref[pair * 2 + ch, 8:rows + 8, :] = mm(x[pair][ch](), spread)
    for img in range(images):
        h_ref[img, 0] = jnp.zeros((160, 256), kind)
        h_ref[img, row_blocks + 1] = jnp.zeros((160, 256), kind)
        c_ref[img, 0] = jnp.zeros((32, 128), jnp.float32)
        c_ref[img, row_blocks + 1] = jnp.zeros((32, 128), jnp.float32)

    strip = lax.broadcasted_iota(jnp.int32, (16, 256), 0)
    first_strip = strip == 0
    last_strip = strip == 15

    def first_layer(step, carry):
        for pair in range(len(x)):
            parts = []
            for ch in range(2):
                for xo in range(4):
                    parts.append(jnp.concatenate([
                        u_ref[pair * 2 + ch, pl.ds(pl.multiple_of((step * FIRST_STEP + k) * 8, 8), 24), xo * 128:(xo + 1) * 128]
                        for k in range(FIRST_STEP)], 1))
            stacked = jnp.concatenate(parts, 0).astype(kind)
            made = mm(stacked, w_first[...], ((0,), (0,)))
            made = jnp.maximum(made + b_first[0:1, :], 0.0)
            for f in range(frames):
                for k in range(FIRST_STEP):
                    for half in range(2):
                        at = f * 512 + half * 256
                        piece = made[k * 128:(k + 1) * 128, at:at + 256]
                        to = h_ref.at[pair * frames + f, 2 * (step * FIRST_STEP + k) + half + 1]
                        to[16:144, :] = piece.astype(kind)
                        to[0:16, :] = jnp.where(first_strip, 0.0, pltpu.roll(piece[112:128], 1, 0)).astype(kind)
                        to[144:160, :] = jnp.where(last_strip, 0.0, pltpu.roll(piece[0:16], 15, 0)).astype(kind)
        return carry

    lax.fori_loop(0, rows // 8 // FIRST_STEP, first_layer, 0)

    n = MID_STEP * 128
    right = (lax.broadcasted_iota(jnp.int32, (n, 256), 1) // 32) % 2 == 1
    right_half = right[:, :128]
    low = lax.broadcasted_iota(jnp.int32, (n, 128), 1) >= 64
    steps = row_blocks // MID_STEP

    def mid_layer(at, carry):
        img, a = at // steps, (at % steps) * MID_STEP

        def part(down, shift, lanes):
            return h_ref[img, pl.ds(a + 1 + down, MID_STEP), 16 + shift:144 + shift, 0:lanes].reshape(n, lanes)

        here = part(0, 0, 256)
        side = jnp.where(right, part(0, -16, 256), part(0, 16, 256))
        across = jnp.where(low, part(-1, 0, 128), part(1, 0, 128))
        corner_left = jnp.where(low, part(-1, -16, 128), part(1, -16, 128))
        corner_right = jnp.where(low, part(-1, 16, 128), part(1, 16, 128))
        corner = jnp.where(right_half, corner_left, corner_right)
        made = mm(jnp.concatenate([here, side, across, corner], 1), w_mid[...])
        hidden = jnp.maximum(made + b_mid[0:1, :], 0.0).astype(kind)
        last = mm(w_last[...], hidden, ((1,), (1,)))
        for k in range(MID_STEP):
            c_ref[img, a + 1 + k] = last[:, k * 128:(k + 1) * 128]
        return carry

    lax.fori_loop(0, images * steps, mid_layer, 0)

    lane = lax.broadcasted_iota(jnp.int32, (row_blocks * 8, 128), 1)
    sub = lax.broadcasted_iota(jnp.int32, (row_blocks * 8, 128), 0) % 8
    half_sub = sub[:row_blocks * 4]

    def moved(value):
        before = jnp.where(lane >= 16, pltpu.roll(value, 16, 1), jnp.where(lane >= 1, pltpu.roll(value, 17, 1), 0.0))
        after = jnp.where(lane < 112, pltpu.roll(value, 112, 1), jnp.where(lane < 127, pltpu.roll(value, 111, 1), 0.0))
        return jnp.where(sub < 4, before, after)

    for img in range(images):

        def piece(at, down=0):
            return c_ref[img, 1 + down:1 + down + row_blocks, at:at + 8, :].reshape(row_blocks * 8, 128)

        total = piece(0) + moved(piece(8))
        edges = piece(16) + moved(piece(24))
        c_ref[img, 1:1 + row_blocks, 16:24, :] = edges.reshape(row_blocks, 8, 128)
        total += jnp.where(sub % 4 == 0, piece(16, -1), 0.0) + jnp.where(sub % 4 == 3, piece(16, 1), 0.0)
        twos = total.reshape(row_blocks // 2, 16, 128)
        even = twos[:, 0:8].reshape(row_blocks * 4, 128)
        odd = twos[:, 8:16].reshape(row_blocks * 4, 128)
        left = jnp.where(half_sub < 4, even, pltpu.roll(odd, 4, 0))
        right_side = jnp.where(half_sub < 4, pltpu.roll(even, rows - 4, 0), odd)
        emit(img // frames, img % frames, mm(jnp.concatenate([left, right_side], 1).astype(kind), gather))


def scratch(pairs, frames, rows):
    images = pairs * frames
    return [
        pltpu.VMEM((192, frames * 512), jnp.bfloat16),
        pltpu.VMEM((8, frames * 512), jnp.float32),
        pltpu.VMEM((768, 256), jnp.bfloat16),
        pltpu.VMEM((8, 256), jnp.float32),
        pltpu.VMEM((32, 256), jnp.bfloat16),
        pltpu.VMEM((32, 512), jnp.float32),
        pltpu.VMEM((pairs * 2, rows + 16, 512), jnp.float32),
        pltpu.VMEM((images, rows // 4 + 2, 160, 256), jnp.bfloat16),
        pltpu.VMEM((images, rows // 4 + 2, 32, 128), jnp.float32),
    ]


def z_kernel(measured, states, response, own, other, cosine, sines, *rest):
    params, tables, spread, gather, data_out, res_out = rest[:5], rest[5:7], rest[7], rest[8], rest[9], rest[10]
    built, work = rest[11:17], rest[17:]
    kind = jnp.bfloat16
    cos, sin = cosine[...], sines[...]
    source = (measured[...] + states[0]).astype(kind)
    row_real = mm(source, cos).astype(kind)
    row_imag = (-mm(source, sin)).astype(kind)
    gain = 1.0 / (1.0 + response[...])
    spec_real = ((mm(cos, row_real) + mm(sin, row_imag)) * gain).astype(kind)
    spec_imag = ((mm(cos, row_imag) - mm(sin, row_real)) * gain).astype(kind)
    back_real = (mm(cos, spec_real) - mm(sin, spec_imag)).astype(kind)
    back_imag = (mm(cos, spec_imag) + mm(sin, spec_real)).astype(kind)
    data_out[...] = (mm(back_real, cos) - mm(back_imag, sin)) * (1.0 / (source.shape[0] * source.shape[1]))

    def emit(pair, f, value):
        res_out[...] = value.astype(kind)

    prepare(0, params, tables, built, 1)
    denoise([(lambda: own[...], lambda: other[...])], built, spread[...], gather[...], emit, *work, frames=1)


def xy_kernel(planes, *rest):
    params, tables, spread, gather, res_out = rest[:5], rest[5:7], rest[7], rest[8], rest[9]
    built, work = rest[10:16], rest[16:]
    for which in range(2):

        def emit(pair, f, value):
            res_out[which, pair, f] = value.astype(jnp.bfloat16)

        pairs = [(lambda p=p: planes[which, p, 0], lambda p=p: planes[which, p, 1]) for p in range(2)]
        prepare(which + 1, params, tables, built, 2)
        denoise(pairs, built, spread[...], gather[...], emit, *work, frames=2)


def final_kernel(states, data, res_z, back_x, back_y, out):
    w = [states[k] for k in range(4)]
    res_x = jnp.transpose(back_x[...].astype(jnp.float32))
    z = [
        2.0 * data[...] - w[0],
        w[1] - 2.0 * res_z[...].astype(jnp.float32),
        w[2] - 2.0 * res_x,
        w[3] - 2.0 * back_y[...].astype(jnp.float32),
    ]
    twice = 0.5 * (z[0] + z[1] + z[2] + z[3])
    for k in range(4):
        out[k] = (1.0 - relaxation) * w[k] + relaxation * (twice - z[k])


VM = pl.BlockSpec(memory_space=pltpu.VMEM)


def call(kernel, out_shape, args, scratch_shapes, flops):
    return pl.pallas_call(
        kernel,
        out_shape=out_shape,
        in_specs=[VM] * len(args),
        out_specs=jax.tree.map(lambda _: VM, out_shape),
        scratch_shapes=scratch_shapes,
        compiler_params=pltpu.CompilerParams(vmem_limit_bytes=56 * 2**20),
        cost_estimate=pl.CostEstimate(flops=flops, bytes_accessed=2**21, transcendentals=0),
    )(*args)


def fourier_tables(length):
    indices = np.arange(length, dtype=np.int32)
    phase = indices[:, None] * indices[None, :] % length
    angle = phase.astype(np.float32) * np.float32(2.0 * math.pi / length)
    return (jnp.asarray(np.cos(angle), jnp.bfloat16), jnp.asarray(np.sin(angle), jnp.bfloat16))


def constants(width):
    kind = jnp.bfloat16
    tables = (first_table(), last_table(), spread_table(width), gather_table(width))
    return tuple(jnp.asarray(table.astype(kind)) for table in tables)


def on_device(states, measured, response, kernel_in, bias_in, kernel_mid, bias_mid, kernel_out):
    kind = jnp.bfloat16
    current = states[:, 0, 0]
    width = current.shape[-1]
    rounded = current[1:].astype(kind)
    devices = lax.axis_size("frame") * lax.axis_size("plane")
    depth = lax.axis_size("plane")
    partner = lax.ppermute(rounded[0], "frame", [(0, 1), (1, 0)])
    leaving = jnp.stack([jnp.transpose(rounded[1]), rounded[2]])
    leaving = leaving.reshape(2, devices, width // devices, width).transpose(1, 0, 2, 3)
    arrived = lax.all_to_all(leaving, ("frame", "plane"), split_axis=0, concat_axis=0, tiled=True)
    planes = arrived.reshape(2, depth, 2, width // devices, width).transpose(2, 3, 0, 1, 4)
    weights = (kernel_in, bias_in, kernel_mid, bias_mid, kernel_out)
    cosine, sines = fourier_tables(width)
    tables = constants(width)
    image = jax.ShapeDtypeStruct((width, width), kind)
    data, res_z = call(
        z_kernel,
        (jax.ShapeDtypeStruct((width, width), jnp.float32), image),
        (measured[0, 0], current, response, rounded[0], partner, cosine, sines) + weights + tables,
        scratch(1, 1, width),
        4 * 10**9,
    )
    residuals = call(
        xy_kernel,
        jax.ShapeDtypeStruct((2, 2, 2, depth, width), kind),
        (planes,) + weights + tables,
        scratch(2, 2, depth),
        8 * 10**9,
    )
    returning = residuals.transpose(2, 3, 0, 1, 4).reshape(devices, 2, width // devices, width)
    returned = lax.all_to_all(returning, ("frame", "plane"), split_axis=0, concat_axis=0, tiled=True)
    returned = returned.transpose(1, 0, 2, 3).reshape(2, width, width)
    out = call(
        final_kernel,
        jax.ShapeDtypeStruct(current.shape, jnp.float32),
        (current, data, res_z, returned[0], returned[1]),
        [],
        10**6,
    )
    return out[:, None, None]


def solution(mesh):
    placed = (
        P(None, "frame", "plane", None, None),
        P("frame", "plane", None, None),
        P(),
        P(),
        P(),
        P(),
        P(),
        P(),
    )
    return jax.shard_map(
        on_device,
        mesh=mesh,
        in_specs=placed,
        out_specs=P(None, "frame", "plane", None, None),
        check_vma=False,
    )
```

time: 146 us -> 69 us (0.47)
  Pallas kernels: 89.4 us -> 34 us
  local copies, waits for them, and re-layouts: 26.5 us -> 7.55 us
  waiting for transfers between devices: 0.01 us -> 6.96 us
  starting transfers between devices: 22.4 us -> 18.3 us
  matrix products: 3.77 us -> 0 us
  other arithmetic: 3.42 us -> 1.65 us
    pallas_call x3, Pallas kernels: 89.4 us -> 34 us  [call(): pl.pallas_call(kernel, out_shape=out_shape, in_specs=[VM] * len(args), ou...]
    transpose x3 -> x0, local copies, waits for them, and re-layouts: 10.1 us -> none  [the longest x1 9.26 us: banded(): jnp.einsum('tsg,dtoc->dscgo', select_mid().astype(kind), kernel_mid[:, 0]...]
    reshape x4 -> x0, local copies, waits for them, and re-layouts: 8.97 us -> none  [the longest x1 6.65 us: banded(): mid = mid.reshape(d, 24 * channels, 8 * channels)]
    all_to_all x1, waiting for transfers between devices: 0.01 us -> 6.95 us  [on_device(): lax.all_to_all(leaving, ('frame', 'plane'), split_axis=0, concat_axis=0,...]
    all_to_all x1, starting transfers between devices: 9.76 us -> 3.86 us  [on_device(): lax.all_to_all(returning, ('frame', 'plane'), split_axis=0, concat_axis=0...]
    dot_general x3 -> x0, matrix products: 3.77 us -> none  [the longest x1 3.14 us: banded(): jnp.einsum('tsg,dtoc->dscgo', select_mid().astype(kind), kernel_mid[:, 0]...]
    all_to_all x1, starting transfers between devices: 8.81 us -> 11.5 us  [on_device(): lax.all_to_all(leaving, ('frame', 'plane'), split_axis=0, concat_axis=0,...]
    convert_element_type x1 -> x0, other arithmetic: 1.73 us -> none  [fourier_tables(): jnp.sin(angle).astype(jnp.bfloat16)]
  transfers between devices with their start and end apart: 3 -> 3, of which waited for: 0 -> 1; matrix products, arithmetic and copies ran while one was open for 21% -> 6% of each run, Pallas kernels for 60% -> 46%
where the time goes in v1:
time: 69 us; the launch traced here: 68.6 us
  Pallas kernels  34 us (49%)
  starting transfers between devices  18.3 us (27%)
  local copies, waits for them, and re-layouts  7.55 us (11%)
  waiting for transfers between devices  6.96 us (10%)
  other arithmetic  1.65 us (2%)
    pallas_call x3, Pallas kernels, call(): pl.pallas_call(kernel, out_shape=out_shape, in_specs=[VM] * len(args), ou...  34 us
    all_to_all x1, starting transfers between devices, on_device(): lax.all_to_all(leaving, ('frame', 'plane'), split_axis=0, concat_axis=0,...  11.5 us
    all_to_all x1, waiting for transfers between devices, on_device(): lax.all_to_all(leaving, ('frame', 'plane'), split_axis=0, concat_axis=0,...  6.95 us
    all_to_all x1, starting transfers between devices, on_device(): lax.all_to_all(returning, ('frame', 'plane'), split_axis=0, concat_axis=0...  3.86 us
    ppermute x1, starting transfers between devices, on_device(): partner = lax.ppermute(rounded[0], 'frame', [(0, 1), (1, 0)])  2.98 us
    unnamed x10, local copies, waits for them, and re-layouts  2.19 us
    reshape x1, local copies, waits for them, and re-layouts, on_device(): residuals.transpose(2, 3, 0, 1, 4)  1.92 us
  transfers between devices with their start and end apart: 3, of which 1 were waited for; matrix products, arithmetic and copies ran while one was open for 6% of the time, Pallas kernels for 46%

profile of v1, /device:TPU:1, one launch (start us, length us, event | category | flops | bytes accessed | tf_op | source)
XLA Modules:
  0.0 68.6 jit_solution(15947325870658727970)
XLA Ops:
  0.0 1.3 %convert.3 = bf16[4,1,1,256,256]{4,3,2,1,0:T(8,128)(2,1)S(1)} convert(f32[4,1,1,256,256]{4,3,2,1,0:T(8,128)} %param.14) | non-fusion elementwise | flops 262144 | bytes 1572864 | tf_op jit(solution)/shard_map/convert
  1.3 0.0 copy-start
  1.3 0.1 copy.33
  1.4 0.1 stack.8
  1.5 0.1 stack.9
  1.6 0.4 maximum_bitcast_fusion
  1.9 0.9 %copy.34 = bf16[128,2,2,256]{3,2,1,0:T(2,128)(2,1)} copy(bf16[128,2,2,256]{3,2,0,1:T(2,128)(2,1)S(1)} %maximum_bitcast_fusion) | data formatting | bytes 524288 | tf_op jit(solution)/shard_map/transpose | solution.py:360
  2.8 0.0 copy-start.2
  2.8 11.5 %all-to-all-start = ((bf16[128,2,2,256]{3,2,1,0:T(2,128)(2,1)}), bf16[128,2,2,256]{3,2,1,0:T(2,128)(2,1)S(1)}, u32[]{:S(2)}, u32[]{:S(2)}) async-start(bf16[128,2,2,256]{3,2,1,0:T(2,128)(2,1)} %copy.34), calls=%async_computation | async-start | bytes 524288 | tf_op jit(solution)/shard_map/all_to_all | solution.py:361
  14.3 0.0 copy-start.1
  14.3 0.0 copy-done
  14.4 3.0 %collective-permute-start = (bf16[256,256]{1,0:T(8,128)(2,1)S(1)}, bf16[256,256]{1,0:T(8,128)(2,1)S(1)}, u32[]{:S(2)}, u32[]{:S(2)}) collective-permute-start(bf16[256,256]{1,0:T(8,128)(2,1)S(1)} %get-tuple-element.11.own), channel_id=1, source_target_pairs={{0,64},{64,0},{1,65},{65,1},{2,66},{66,2},{3,67},{67,3},{4,68},{68... | collective-permute-start | bytes 393224 | tf_op jit(solution)/shard_map/ppermute | solution.py:358
  17.3 0.0 copy-done.2
  17.3 0.6 copy.32.rest_4_
  17.9 0.0 copy-done.1
  17.9 0.9 %copy.31.rest_0_ = bf16[3,9,32,2]{3,2,1,0:T(8,128)(2,1)} copy(bf16[3,9,32,2]{2,3,1,0:T(2,128)(2,1)S(1)} %copy-done.1) | data formatting | bytes 6912 | tf_op args[3]
  18.9 7.0 %all-to-all-done = bf16[128,2,2,256]{3,2,1,0:T(2,128)(2,1)S(1)} async-done(((bf16[128,2,2,256]{3,2,1,0:T(2,128)(2,1)}), bf16[128,2,2,256]{3,2,1,0:T(2,128)(2,1)S(1)}, u32[]{:S(2)}, u32[]{:S(2)}) %all-to-all-start) | async-done | bytes 262176 | tf_op jit(solution)/shard_map/all_to_all | solution.py:361
  25.8 0.7 %copy.35 = bf16[128,2,2,256]{3,0,2,1:T(8,128)(2,1)} copy(bf16[128,2,2,256]{3,2,1,0:T(2,128)(2,1)S(1)} %all-to-all-done) | data formatting | bytes 524288 | tf_op jit(solution)/shard_map/all_to_all | solution.py:361
  26.6 18.9 %shard_map.137 = bf16[2,2,2,64,256]{4,3,2,1,0:T(8,128)(2,1)} custom-call(bf16[2,2,2,64,256]{4,3,2,1,0:T(8,128)(2,1)} %bitcast.29, bf16[3,9,32,2]{3,2,1,0:T(8,128)(2,1)} %copy.31.rest_0_, f32[3,32]{1,0:T(4,128)} %rest_1_.3, bf16[3,1,9,32,32]{4,3,2,1,0:T(8,128)(2,1)} %rest_2_.3, f32[3,1,32]{2,1,0:T(1,128)} %rest_3_.3, bf16[3,9,32]{2,1,0:T(8,128)(2,1)} %copy.32.rest_4_, ...), custom_call_target="tpu_custom_call" | custom-call | flops 8000000000 | bytes 2097152 | tf_op jit(solution)/shard_map/pallas_call | solution.py:327
  45.5 1.9 %copy.38 = bf16[128,2,2,256]{3,2,1,0:T(2,128)(2,1)} copy(bf16[128,2,2,256]{3,0,2,1:T(8,128)(2,1)} %bitcast.30) | data formatting | bytes 524288 | tf_op jit(solution)/shard_map/reshape | solution.py:381
  47.4 3.9 %all-to-all-start.1 = ((bf16[128,2,2,256]{3,2,1,0:T(2,128)(2,1)}), bf16[128,2,2,256]{3,2,1,0:T(2,128)(2,1)S(1)}, u32[]{:S(2)}, u32[]{:S(2)}) async-start(bf16[128,2,2,256]{3,2,1,0:T(2,128)(2,1)} %copy.38), calls=%async_computation.1 | async-start | bytes 524288 | tf_op jit(solution)/shard_map/all_to_all | solution.py:382
  51.3 0.0 collective-permute-done.other
  51.3 0.0 copy-start.3
  51.3 0.6 copy-done.3
  51.9 12.4 %shard_map.136 = (f32[256,256]{1,0:T(8,128)}, bf16[256,256]{1,0:T(8,128)(2,1)}) custom-call(f32[256,256]{1,0:T(8,128)} %bitcast.31, f32[4,256,256]{2,1,0:T(8,128)} %bitcast.26, f32[256,256]{1,0:T(8,128)} %response.1, bf16[256,256]{1,0:T(8,128)(2,1)} %copy-done, bf16[256,256]{1,0:T(8,128)(2,1)} %copy-done.3, bf16[256,256]{1,0:T(8,128)(2,1)} %constant.12.clone.cosine, ...), custom_call_target="tpu_custom_call" | custom-call | flops 4000000000 | bytes 2097152 | tf_op jit(solution)/shard_map/pallas_call | solution.py:327
  64.3 0.0 all-to-all-done.1
  64.4 0.2 fusion
  64.5 0.7 %squeeze.24.back_y = bf16[256,256]{1,0:T(8,128)(2,1)} reshape(bf16[1,128,2,256]{3,2,0,1:T(2,128)(2,1)S(1)} %get-tuple-element.12) | data formatting | bytes 262144 | tf_op jit(solution)/shard_map/squeeze | solution.py:387
  65.2 0.7 %squeeze.23.back_x = bf16[256,256]{1,0:T(8,128)(2,1)} reshape(bf16[1,128,2,256]{3,2,0,1:T(2,128)(2,1)S(1)} %get-tuple-element.13) | data formatting | bytes 262144 | tf_op jit(solution)/shard_map/squeeze | solution.py:387
  65.9 2.7 %shard_map.138 = f32[4,256,256]{2,1,0:T(8,128)} custom-call(f32[4,256,256]{2,1,0:T(8,128)} %bitcast.27, f32[256,256]{1,0:T(8,128)} %get-tuple-element.7.data, bf16[256,256]{1,0:T(8,128)(2,1)} %get-tuple-element.8.res_z, bf16[256,256]{1,0:T(8,128)(2,1)} %squeeze.23.back_x, bf16[256,256]{1,0:T(8,128)(2,1)} %squeeze.24.back_y), custom_call_target="tpu_custom_call" | custom-call | flops 1000000 | bytes 2097152 | tf_op jit(solution)/shard_map/pallas_call | solution.py:327
  (1 shorter events, 0.0 us)
Async XLA Ops:
  1.3 13.0 %copy-start = (bf16[256,256]{1,0:T(8,128)(2,1)}, bf16[256,256]{1,0:T(8,128)(2,1)S(1)}, u32[]{:S(2)}) copy-start(bf16[256,256]{1,0:T(8,128)(2,1)S(1)} %get-tuple-element.11.own) | copy-start | bytes 393220
  2.8 14.5 %copy-start.2 = (bf16[3,9,32]{2,0,1:T(4,128)(2,1)S(1)}, bf16[3,9,32]{2,0,1:T(4,128)(2,1)}, u32[]{:S(2)}) copy-start(bf16[3,9,32]{2,0,1:T(4,128)(2,1)} %param.21) | copy-start | bytes 5188
  2.8 23.0 %all-to-all-start = ((bf16[128,2,2,256]{3,2,1,0:T(2,128)(2,1)}), bf16[128,2,2,256]{3,2,1,0:T(2,128)(2,1)S(1)}, u32[]{:S(2)}, u32[]{:S(2)}) async-start(bf16[128,2,2,256]{3,2,1,0:T(2,128)(2,1)} %copy.34), calls=%async_computation | async-start | bytes 524288 | tf_op jit(solution)/shard_map/all_to_all | solution.py:361
  14.3 3.6 %copy-start.1 = (bf16[3,9,32,2]{2,3,1,0:T(2,128)(2,1)S(1)}, bf16[3,9,32,2]{2,3,1,0:T(2,128)(2,1)}, u32[]{:S(2)}) copy-start(bf16[3,9,32,2]{2,3,1,0:T(2,128)(2,1)} %param.17) | copy-start | bytes 10372
  14.4 36.9 %collective-permute-start = (bf16[256,256]{1,0:T(8,128)(2,1)S(1)}, bf16[256,256]{1,0:T(8,128)(2,1)S(1)}, u32[]{:S(2)}, u32[]{:S(2)}) collective-permute-start(bf16[256,256]{1,0:T(8,128)(2,1)S(1)} %get-tuple-element.11.own), channel_id=1, source_target_pairs={{0,64},{64,0},{1,65},{65,1},{2,66},{66,2},{3,67},{67,3},{4,68},{68... | collective-permute-start | bytes 393224 | tf_op jit(solution)/shard_map/ppermute | solution.py:358
  47.4 17.0 %all-to-all-start.1 = ((bf16[128,2,2,256]{3,2,1,0:T(2,128)(2,1)}), bf16[128,2,2,256]{3,2,1,0:T(2,128)(2,1)S(1)}, u32[]{:S(2)}, u32[]{:S(2)}) async-start(bf16[128,2,2,256]{3,2,1,0:T(2,128)(2,1)} %copy.38), calls=%async_computation.1 | async-start | bytes 524288 | tf_op jit(solution)/shard_map/all_to_all | solution.py:382
  51.3 0.7 copy-start.3

commit v2 on v1

--- a/solution.py
+++ b/solution.py
@@ -10,6 +10,8 @@
 from jax.sharding import PartitionSpec as P
 
 relaxation = 0.8
+MESH = pl.DeviceIdType.MESH
+UNROLL = 8
 
 GROUPS = [(0, 0), (0, 1), (3, 0), (3, 1), (1, 0), (1, 1), (2, 0), (2, 1)]
 STRIP = 16
@@ -158,8 +160,8 @@
     w_last[...] = mm(last_at[...], jnp.where(own, tiled, 0.0).astype(kind)).astype(kind)
 
 
-def denoise(x, built, spread, gather, emit, u_ref, h_ref, c_ref, frames):
-    w_first, b_first, w_mid, b_mid, w_last, _ = built
+def first_half(x, built, spread, u_ref, h_ref, c_ref, frames):
+    w_first, b_first = built[:2]
     rows = u_ref.shape[1] - 16
     row_blocks = rows // 4
     images = len(x) * frames
@@ -203,6 +205,13 @@
 
     lax.fori_loop(0, rows // 8 // FIRST_STEP, first_layer, 0)
 
+
+def second_half(built, gather, emit, h_ref, c_ref, frames):
+    w_mid, b_mid, w_last = built[2:5]
+    images = h_ref.shape[0]
+    row_blocks = h_ref.shape[1] - 2
+    rows = row_blocks * 4
+    kind = jnp.bfloat16
     n = MID_STEP * 128
     right = (lax.broadcasted_iota(jnp.int32, (n, 256), 1) // 32) % 2 == 1
     right_half = right[:, :128]
@@ -256,8 +265,7 @@
         emit(img // frames, img % frames, mm(jnp.concatenate([left, right_side], 1).astype(kind), gather))
 
 
-def scratch(pairs, frames, rows):
-    images = pairs * frames
+def built_shapes(frames):
     return [
         pltpu.VMEM((192, frames * 512), jnp.bfloat16),
         pltpu.VMEM((8, frames * 512), jnp.float32),
@@ -265,74 +273,145 @@
         pltpu.VMEM((8, 256), jnp.float32),
         pltpu.VMEM((32, 256), jnp.bfloat16),
         pltpu.VMEM((32, 512), jnp.float32),
+    ]
+
+
+def work_shapes(pairs, frames, rows):
+    images = pairs * frames
+    return [
         pltpu.VMEM((pairs * 2, rows + 16, 512), jnp.float32),
         pltpu.VMEM((images, rows // 4 + 2, 160, 256), jnp.bfloat16),
         pltpu.VMEM((images, rows // 4 + 2, 32, 128), jnp.float32),
     ]
 
 
-def z_kernel(measured, states, response, own, other, cosine, sines, *rest):
-    params, tables, spread, gather, data_out, res_out = rest[:5], rest[5:7], rest[7], rest[8], rest[9], rest[10]
-    built, work = rest[11:17], rest[17:]
-    kind = jnp.bfloat16
-    cos, sin = cosine[...], sines[...]
-    source = (measured[...] + states[0]).astype(kind)
+def filtered(source, response, cos, sin):
+    kind = jnp.bfloat16
     row_real = mm(source, cos).astype(kind)
     row_imag = (-mm(source, sin)).astype(kind)
-    gain = 1.0 / (1.0 + response[...])
+    gain = 1.0 / (1.0 + response)
     spec_real = ((mm(cos, row_real) + mm(sin, row_imag)) * gain).astype(kind)
     spec_imag = ((mm(cos, row_imag) - mm(sin, row_real)) * gain).astype(kind)
     back_real = (mm(cos, spec_real) - mm(sin, spec_imag)).astype(kind)
     back_imag = (mm(cos, spec_imag) + mm(sin, spec_real)).astype(kind)
-    data_out[...] = (mm(back_real, cos) - mm(back_imag, sin)) * (1.0 / (source.shape[0] * source.shape[1]))
-
-    def emit(pair, f, value):
-        res_out[...] = value.astype(kind)
-
-    prepare(0, params, tables, built, 1)
-    denoise([(lambda: own[...], lambda: other[...])], built, spread[...], gather[...], emit, *work, frames=1)
-
-
-def xy_kernel(planes, *rest):
-    params, tables, spread, gather, res_out = rest[:5], rest[5:7], rest[7], rest[8], rest[9]
-    built, work = rest[10:16], rest[16:]
+    return (mm(back_real, cos) - mm(back_imag, sin)) * (1.0 / (source.shape[0] * source.shape[1]))
+
+
+def whole_kernel(depth, states, measured, response, cosine, sines, *rest):
+    params, tables, spread, gather, out = rest[:5], rest[5:7], rest[7], rest[8], rest[9]
+    built = [rest[10:16], rest[16:22], rest[22:28]]
+    z_work, xy_work = rest[28:31], rest[31:34]
+    z_own, z_other, turned, data, z_res, leaving, arrived, going, returned = rest[34:43]
+    z_send, z_recv, there_send, there_recv, back_send, back_recv = rest[43:]
+    kind = jnp.bfloat16
+    devices = 2 * depth
+    frame = lax.axis_index("frame")
+    plane = lax.axis_index("plane")
+    me = frame * depth + plane
+
+    def at(k):
+        other = me ^ k
+        return other, (other // depth, other % depth)
+
+    barrier = pltpu.get_barrier_semaphore()
+
+    def greet(k, carry):
+        pl.semaphore_signal(barrier, inc=1, device_id=at(k)[1], device_id_type=MESH)
+        return carry
+
+    lax.fori_loop(1, devices, greet, 0, unroll=UNROLL)
+
+    z_own[...] = states[1].astype(kind)
+    for which, value in enumerate((jnp.transpose(states[2]), states[3])):
+        for half in range(2):
+            turned[which * 2 + half] = value[:, half * 128:(half + 1) * 128]
+        for p in range(2):
+            for half in range(2):
+                leaving[pl.ds(which * 4 + p * 2 + half, devices, stride=8), :] = turned[which * 2 + half, pl.ds(p, devices, stride=2), :]
+    prepare(0, params, tables, built[0], 1)
+    pl.semaphore_wait(barrier, devices - 1)
+
+    def packet(ref, d):
+        return ref.at[pl.ds(pl.multiple_of(d * 8, 8), 8), :]
+
+    def exchange(source, target, send, recv):
+        pltpu.make_async_copy(packet(source, me), packet(target, me), recv).start()
+
+        def go(k, carry):
+            other, coordinates = at(k)
+            pltpu.make_async_remote_copy(
+                src_ref=packet(source, other),
+                dst_ref=packet(target, me),
+                send_sem=send,
+                recv_sem=recv,
+                device_id=coordinates,
+                device_id_type=MESH,
+            ).start()
+            return carry
+
+        lax.fori_loop(1, devices, go, 0, unroll=UNROLL)
+
+    def all_sent(source, send):
+        some = source.at[pl.ds(0, (devices - 1) * 8), :]
+        pltpu.make_async_copy(some, some, send).wait()
+
+    def all_here(target, recv):
+        pltpu.make_async_copy(target, target, recv).wait()
+
+    swap = pltpu.make_async_remote_copy(
+        src_ref=z_own, dst_ref=z_other, send_sem=z_send, recv_sem=z_recv,
+        device_id=(1 - frame, plane), device_id_type=MESH,
+    )
+    swap.start()
+    exchange(leaving, arrived, there_send, there_recv)
+
+    prepare(1, params, tables, built[1], 2)
+    prepare(2, params, tables, built[2], 2)
+    source = (measured[...] + states[0]).astype(kind)
+    data[...] = filtered(source, response[...], cosine[...], sines[...])
+    swap.wait()
+    first_half([(lambda: z_own[...], lambda: z_other[...])], built[0], spread[...], *z_work, frames=1)
+
+    all_here(arrived, there_recv)
+    all_sent(leaving, there_send)
+
+    def rows_of(which, p, f, half):
+        return pl.ds(f * depth * 8 + which * 4 + p * 2 + half, depth, stride=8)
+
     for which in range(2):
 
-        def emit(pair, f, value):
-            res_out[which, pair, f] = value.astype(jnp.bfloat16)
-
-        pairs = [(lambda p=p: planes[which, p, 0], lambda p=p: planes[which, p, 1]) for p in range(2)]
-        prepare(which + 1, params, tables, built, 2)
-        denoise(pairs, built, spread[...], gather[...], emit, *work, frames=2)
-
-
-def final_kernel(states, data, res_z, back_x, back_y, out):
+        def plane_of(p, f):
+            return jnp.concatenate([arrived[rows_of(which, p, f, half), :] for half in range(2)], 1).astype(kind)
+
+        def emit(p, f, value):
+            for half in range(2):
+                going[rows_of(which, p, f, half), :] = value[:, half * 128:(half + 1) * 128]
+
+        pairs = [(functools.partial(plane_of, p, 0), functools.partial(plane_of, p, 1)) for p in range(2)]
+        first_half(pairs, built[which + 1], spread[...], *xy_work, frames=2)
+        second_half(built[which + 1], gather[...], emit, *xy_work[1:], frames=2)
+    exchange(going, returned, back_send, back_recv)
+
+    def emit_z(p, f, value):
+        z_res[...] = value
+
+    second_half(built[0], gather[...], emit_z, *z_work[1:], frames=1)
+    all_here(returned, back_recv)
+    all_sent(going, back_send)
+
+    def unpack(which):
+        for p in range(2):
+            for half in range(2):
+                turned[which * 2 + half, pl.ds(p, devices, stride=2), :] = returned[pl.ds(which * 4 + p * 2 + half, devices, stride=8), :]
+        return jnp.concatenate([turned[which * 2], turned[which * 2 + 1]], 1)
+
+    res_x = jnp.transpose(unpack(0))
+    res_y = unpack(1)
     w = [states[k] for k in range(4)]
-    res_x = jnp.transpose(back_x[...].astype(jnp.float32))
-    z = [
-        2.0 * data[...] - w[0],
-        w[1] - 2.0 * res_z[...].astype(jnp.float32),
-        w[2] - 2.0 * res_x,
-        w[3] - 2.0 * back_y[...].astype(jnp.float32),
-    ]
+    z = [2.0 * data[...] - w[0], w[1] - 2.0 * z_res[...], w[2] - 2.0 * res_x, w[3] - 2.0 * res_y]
     twice = 0.5 * (z[0] + z[1] + z[2] + z[3])
     for k in range(4):
         out[k] = (1.0 - relaxation) * w[k] + relaxation * (twice - z[k])
-
-
-VM = pl.BlockSpec(memory_space=pltpu.VMEM)
-
-
-def call(kernel, out_shape, args, scratch_shapes, flops):
-    return pl.pallas_call(
-        kernel,
-        out_shape=out_shape,
-        in_specs=[VM] * len(args),
-        out_specs=jax.tree.map(lambda _: VM, out_shape),
-        scratch_shapes=scratch_shapes,
-        compiler_params=pltpu.CompilerParams(vmem_limit_bytes=56 * 2**20),
-        cost_estimate=pl.CostEstimate(flops=flops, bytes_accessed=2**21, transcendentals=0),
-    )(*args)
 
 
 def fourier_tables(length):
@@ -349,45 +428,26 @@
 
 
 def on_device(states, measured, response, kernel_in, bias_in, kernel_mid, bias_mid, kernel_out):
-    kind = jnp.bfloat16
     current = states[:, 0, 0]
     width = current.shape[-1]
-    rounded = current[1:].astype(kind)
-    devices = lax.axis_size("frame") * lax.axis_size("plane")
     depth = lax.axis_size("plane")
-    partner = lax.ppermute(rounded[0], "frame", [(0, 1), (1, 0)])
-    leaving = jnp.stack([jnp.transpose(rounded[1]), rounded[2]])
-    leaving = leaving.reshape(2, devices, width // devices, width).transpose(1, 0, 2, 3)
-    arrived = lax.all_to_all(leaving, ("frame", "plane"), split_axis=0, concat_axis=0, tiled=True)
-    planes = arrived.reshape(2, depth, 2, width // devices, width).transpose(2, 3, 0, 1, 4)
-    weights = (kernel_in, bias_in, kernel_mid, bias_mid, kernel_out)
-    cosine, sines = fourier_tables(width)
-    tables = constants(width)
-    image = jax.ShapeDtypeStruct((width, width), kind)
-    data, res_z = call(
-        z_kernel,
-        (jax.ShapeDtypeStruct((width, width), jnp.float32), image),
-        (measured[0, 0], current, response, rounded[0], partner, cosine, sines) + weights + tables,
-        scratch(1, 1, width),
-        4 * 10**9,
-    )
-    residuals = call(
-        xy_kernel,
-        jax.ShapeDtypeStruct((2, 2, 2, depth, width), kind),
-        (planes,) + weights + tables,
-        scratch(2, 2, depth),
-        8 * 10**9,
-    )
-    returning = residuals.transpose(2, 3, 0, 1, 4).reshape(devices, 2, width // devices, width)
-    returned = lax.all_to_all(returning, ("frame", "plane"), split_axis=0, concat_axis=0, tiled=True)
-    returned = returned.transpose(1, 0, 2, 3).reshape(2, width, width)
-    out = call(
-        final_kernel,
-        jax.ShapeDtypeStruct(current.shape, jnp.float32),
-        (current, data, res_z, returned[0], returned[1]),
-        [],
-        10**6,
-    )
+    args = (current, measured[0, 0], response) + fourier_tables(width)
+    args += (kernel_in, bias_in, kernel_mid, bias_mid, kernel_out) + constants(width)
+    image = pltpu.VMEM((width, width), jnp.float32)
+    short = pltpu.VMEM((width, width), jnp.bfloat16)
+    packets = pltpu.VMEM((2 * depth * 8, 128), jnp.float32)
+    out = pl.pallas_call(
+        functools.partial(whole_kernel, depth),
+        out_shape=jax.ShapeDtypeStruct(current.shape, jnp.float32),
+        in_specs=[pl.BlockSpec(memory_space=pltpu.VMEM)] * len(args),
+        out_specs=pl.BlockSpec(memory_space=pltpu.VMEM),
+        scratch_shapes=built_shapes(1) + built_shapes(2) + built_shapes(2)
+        + work_shapes(1, 1, width) + work_shapes(2, 2, depth)
+        + [short, short, pltpu.VMEM((4, width, 128), jnp.float32), image, image, packets, packets, packets, packets]
+        + [pltpu.SemaphoreType.DMA] * 6,
+        compiler_params=pltpu.CompilerParams(vmem_limit_bytes=60 * 2**20, collective_id=0, has_side_effects=True),
+        cost_estimate=pl.CostEstimate(flops=12 * 10**9, bytes_accessed=2**22, transcendentals=0),
+    )(*args)
     return out[:, None, None]
 
 

time: 69 us -> 59.9 us (0.87)
  Pallas kernels: 34 us -> 55.1 us
  starting transfers between devices: 18.3 us -> 0 us
  waiting for transfers between devices: 6.96 us -> 0 us
  local copies, waits for them, and re-layouts: 7.55 us -> 4.53 us
  other arithmetic: 1.65 us -> 0 us
    pallas_call x3 -> x1, Pallas kernels: 34 us -> 55.1 us  [on_device(): pl.pallas_call(functools.partial(whole_kernel, depth), out_shape=jax.Shap...]
    all_to_all x2 -> x0, starting transfers between devices: 15.4 us -> none  [the longest x1 11.5 us: on_device(): lax.all_to_all(leaving, ('frame', 'plane'), split_axis=0, concat_axis=0,...]
    all_to_all x2 -> x0, waiting for transfers between devices: 6.96 us -> none  [the longest x1 6.95 us: on_device(): lax.all_to_all(leaving, ('frame', 'plane'), split_axis=0, concat_axis=0,...]
    ppermute x1 -> x0, starting transfers between devices: 2.98 us -> none  [on_device(): partner = lax.ppermute(rounded[0], 'frame', [(0, 1), (1, 0)])]
    unnamed x10 -> x5, local copies, waits for them, and re-layouts: 2.19 us -> 4.53 us
    reshape x1 -> x0, local copies, waits for them, and re-layouts: 1.92 us -> none  [on_device(): residuals.transpose(2, 3, 0, 1, 4)]
    squeeze x2 -> x0, local copies, waits for them, and re-layouts: 1.4 us -> none  [the longest x1 0.7 us: on_device(): returned[0]]
    another operation x1 -> x0, other arithmetic: 1.28 us -> none
  transfers between devices with their start and end apart: 3 -> 0, of which waited for: 1 -> 0; matrix products, arithmetic and copies ran while one was open for 6% -> 0% of each run, Pallas kernels for 46% -> 0%
where the time goes in v2:
time: 59.9 us; the launch traced here: 59.7 us
  Pallas kernels  55.1 us (92%)
  local copies, waits for them, and re-layouts  4.53 us (8%)
    pallas_call x1, Pallas kernels, on_device(): pl.pallas_call(functools.partial(whole_kernel, depth), out_shape=jax.Shap...  55.1 us
    unnamed x5, local copies, waits for them, and re-layouts  4.53 us

profile of v2, /device:TPU:1, one launch (start us, length us, event | category | flops | bytes accessed | tf_op | source)
XLA Modules:
  0.0 59.7 jit_solution(9223204576273125288)
XLA Ops:
  0.0 0.0 copy-start
  0.0 1.3 %copy.16.rest_4_ = bf16[3,9,32]{2,1,0:T(8,128)(2,1)} copy(bf16[3,9,32]{2,0,1:T(4,128)(2,1)} %param.21) | data formatting | bytes 3456 | tf_op args[7]
  1.3 0.0 copy-done
  1.3 0.9 %copy.15.rest_0_ = bf16[3,9,32,2]{3,2,1,0:T(8,128)(2,1)} copy(bf16[3,9,32,2]{2,3,1,0:T(2,128)(2,1)S(1)} %copy-done) | data formatting | bytes 6912 | tf_op args[3]
  2.2 55.1 %shard_map.136 = f32[4,256,256]{2,1,0:T(8,128)} custom-call(f32[4,256,256]{2,1,0:T(8,128)} %bitcast.6, f32[256,256]{1,0:T(8,128)} %bitcast.7, f32[256,256]{1,0:T(8,128)} %response.1, bf16[256,256]{1,0:T(8,128)(2,1)} %constant.12.clone.cosine, bf16[256,256]{1,0:T(8,128)(2,1)} %constant.13.clone.sines, bf16[3,9,32,2]{3,2,1,0:T(8,128)(2,1)} %copy.15.rest_0_, ...), custom_call_target="tpu_custom_call" | custom-call | flops 12000000000 | bytes 4194304 | tf_op jit(solution)/shard_map/pallas_call | solution.py:439
  57.4 2.3 %copy.19 = f32[4,1,1,256,256]{4,3,2,1,0:T(8,128)} copy(f32[4,1,1,256,256]{4,3,2,1,0:T(8,128)} %bitcast.5) | data formatting | bytes 2097152
Async XLA Ops:
  0.0 1.3 %copy-start = (bf16[3,9,32,2]{2,3,1,0:T(2,128)(2,1)S(1)}, bf16[3,9,32,2]{2,3,1,0:T(2,128)(2,1)}, u32[]{:S(2)}) copy-start(bf16[3,9,32,2]{2,3,1,0:T(2,128)(2,1)} %param.17) | copy-start | bytes 10372

commit v3 on v2

--- a/solution.py
+++ b/solution.py
@@ -129,7 +129,7 @@
 
     spare[...] = jnp.zeros_like(spare)
     for tap in range(9):
-        spare[2 * tap:2 * tap + 2, :] = mm(kernel_in[d, tap], wide, ((0,), (0,)))
+        spare[2 * tap:2 * tap + 2, :] = mm(kernel_in[d, tap], wide)
     tiled = jnp.concatenate([spare[...]] * 16, 0)
     own = lax.broadcasted_iota(jnp.int32, (512, 512), 0) // 32 == lax.broadcasted_iota(jnp.int32, (512, 512), 1) // 32
     built_first = mm(first_at[...], jnp.where(own, tiled, 0.0).astype(kind)).astype(kind)
@@ -154,7 +154,7 @@
         w_mid[s * 32:(s + 1) * 32, :] = value.astype(kind)
 
     spare[9:16, 0:256] = jnp.zeros((7, 256), jnp.float32)
-    spare[0:9, 0:256] = mm(kernel_out[d], narrow)
+    spare[0:9, 0:256] = mm(kernel_out[:, d, :], narrow)
     tiled = jnp.concatenate([spare[0:16, 0:256]] * 8, 0)
     own = lax.broadcasted_iota(jnp.int32, (128, 256), 0) // 16 == lax.broadcasted_iota(jnp.int32, (128, 256), 1) // 32
     w_last[...] = mm(last_at[...], jnp.where(own, tiled, 0.0).astype(kind)).astype(kind)
@@ -297,12 +297,15 @@
     return (mm(back_real, cos) - mm(back_imag, sin)) * (1.0 / (source.shape[0] * source.shape[1]))
 
 
-def whole_kernel(depth, states, measured, response, cosine, sines, *rest):
-    params, tables, spread, gather, out = rest[:5], rest[5:7], rest[7], rest[8], rest[9]
-    built = [rest[10:16], rest[16:22], rest[22:28]]
-    z_work, xy_work = rest[28:31], rest[31:34]
-    z_own, z_other, turned, data, z_res, leaving, arrived, going, returned = rest[34:43]
-    z_send, z_recv, there_send, there_recv, back_send, back_recv = rest[43:]
+def whole_kernel(depth, states_at, measured_at, response_at, cosine_at, sines_at, *rest):
+    params, tables, spread, gather = rest[:5], rest[5:7], rest[7], rest[8]
+    data, z_res, x_res, y_res = rest[9:13]
+    rest = rest[13:]
+    built = [rest[0:6], rest[6:12], rest[12:18]]
+    z_work, xy_work = rest[18:21], rest[21:24]
+    z_own, z_other, turned, rows_f32, leaving, arrived, going, returned = rest[24:32]
+    states, measured, response, cosine, sines, loaded = rest[32:38]
+    z_send, z_recv, there_send, there_recv, back_send, back_recv = rest[38:]
     kind = jnp.bfloat16
     devices = 2 * depth
     frame = lax.axis_index("frame")
@@ -319,20 +322,29 @@
         pl.semaphore_signal(barrier, inc=1, device_id=at(k)[1], device_id_type=MESH)
         return carry
 
+    loads = [pltpu.make_async_copy(states_at.at[k], states.at[k], loaded.at[k]) for k in range(4)]
+    for k, (source, target) in enumerate(((measured_at, measured), (response_at, response), (cosine_at, cosine), (sines_at, sines))):
+        loads.append(pltpu.make_async_copy(source, target, loaded.at[4 + k]))
+    for k in (2, 3, 1, 0, 4, 5, 6, 7):
+        loads[k].start()
     lax.fori_loop(1, devices, greet, 0, unroll=UNROLL)
 
-    z_own[...] = states[1].astype(kind)
+    loads[2].wait()
+    loads[3].wait()
     for which, value in enumerate((jnp.transpose(states[2]), states[3])):
         for half in range(2):
             turned[which * 2 + half] = value[:, half * 128:(half + 1) * 128]
         for p in range(2):
             for half in range(2):
-                leaving[pl.ds(which * 4 + p * 2 + half, devices, stride=8), :] = turned[which * 2 + half, pl.ds(p, devices, stride=2), :]
+                rows_f32[pl.ds(which * 4 + p * 2 + half, devices, stride=8), :] = turned[which * 2 + half, pl.ds(p, devices, stride=2), :]
+    leaving[...] = rows_f32[...].reshape(devices, 8, 128).astype(kind)
+    loads[1].wait()
+    z_own[...] = states[1].astype(kind)
     prepare(0, params, tables, built[0], 1)
     pl.semaphore_wait(barrier, devices - 1)
 
     def packet(ref, d):
-        return ref.at[pl.ds(pl.multiple_of(d * 8, 8), 8), :]
+        return ref.at[d]
 
     def exchange(source, target, send, recv):
         pltpu.make_async_copy(packet(source, me), packet(target, me), recv).start()
@@ -352,7 +364,7 @@
         lax.fori_loop(1, devices, go, 0, unroll=UNROLL)
 
     def all_sent(source, send):
-        some = source.at[pl.ds(0, (devices - 1) * 8), :]
+        some = source.at[pl.ds(0, devices - 1)]
         pltpu.make_async_copy(some, some, send).wait()
 
     def all_here(target, recv):
@@ -367,6 +379,8 @@
 
     prepare(1, params, tables, built[1], 2)
     prepare(2, params, tables, built[2], 2)
+    for k in (0, 4, 5, 6, 7):
+        loads[k].wait()
     source = (measured[...] + states[0]).astype(kind)
     data[...] = filtered(source, response[...], cosine[...], sines[...])
     swap.wait()
@@ -374,6 +388,7 @@
 
     all_here(arrived, there_recv)
     all_sent(leaving, there_send)
+    rows_f32[...] = arrived[...].astype(jnp.float32).reshape(devices * 8, 128)
 
     def rows_of(which, p, f, half):
         return pl.ds(f * depth * 8 + which * 4 + p * 2 + half, depth, stride=8)
@@ -381,34 +396,41 @@
     for which in range(2):
 
         def plane_of(p, f):
-            return jnp.concatenate([arrived[rows_of(which, p, f, half), :] for half in range(2)], 1).astype(kind)
+            return jnp.concatenate([rows_f32[rows_of(which, p, f, half), :] for half in range(2)], 1).astype(kind)
 
         def emit(p, f, value):
             for half in range(2):
-                going[rows_of(which, p, f, half), :] = value[:, half * 128:(half + 1) * 128]
+                rows_f32[rows_of(which, p, f, half), :] = value[:, half * 128:(half + 1) * 128]
 
         pairs = [(functools.partial(plane_of, p, 0), functools.partial(plane_of, p, 1)) for p in range(2)]
         first_half(pairs, built[which + 1], spread[...], *xy_work, frames=2)
         second_half(built[which + 1], gather[...], emit, *xy_work[1:], frames=2)
+    going[...] = rows_f32[...].reshape(devices, 8, 128).astype(kind)
     exchange(going, returned, back_send, back_recv)
 
     def emit_z(p, f, value):
-        z_res[...] = value
+        z_res[...] = value.astype(kind)
 
     second_half(built[0], gather[...], emit_z, *z_work[1:], frames=1)
     all_here(returned, back_recv)
     all_sent(going, back_send)
 
+    rows_f32[...] = returned[...].astype(jnp.float32).reshape(devices * 8, 128)
+
     def unpack(which):
         for p in range(2):
             for half in range(2):
-                turned[which * 2 + half, pl.ds(p, devices, stride=2), :] = returned[pl.ds(which * 4 + p * 2 + half, devices, stride=8), :]
+                turned[which * 2 + half, pl.ds(p, devices, stride=2), :] = rows_f32[pl.ds(which * 4 + p * 2 + half, devices, stride=8), :]
         return jnp.concatenate([turned[which * 2], turned[which * 2 + 1]], 1)
 
-    res_x = jnp.transpose(unpack(0))
-    res_y = unpack(1)
+    x_res[...] = jnp.transpose(unpack(0)).astype(kind)
+    y_res[...] = unpack(1).astype(kind)
+
+
+def final_kernel(states, data, res_z, res_x, res_y, out):
     w = [states[k] for k in range(4)]
-    z = [2.0 * data[...] - w[0], w[1] - 2.0 * z_res[...], w[2] - 2.0 * res_x, w[3] - 2.0 * res_y]
+    z = [2.0 * data[...] - w[0]]
+    z += [w[k + 1] - 2.0 * res[...].astype(jnp.float32) for k, res in enumerate((res_z, res_x, res_y))]
     twice = 0.5 * (z[0] + z[1] + z[2] + z[3])
     for k in range(4):
         out[k] = (1.0 - relaxation) * w[k] + relaxation * (twice - z[k])
@@ -431,23 +453,39 @@
     current = states[:, 0, 0]
     width = current.shape[-1]
     depth = lax.axis_size("plane")
+    kind = jnp.bfloat16
     args = (current, measured[0, 0], response) + fourier_tables(width)
-    args += (kernel_in, bias_in, kernel_mid, bias_mid, kernel_out) + constants(width)
+    args += (jnp.transpose(kernel_in, (0, 1, 3, 2)), bias_in, kernel_mid, bias_mid, jnp.transpose(kernel_out, (1, 0, 2))) + constants(width)
+    short = pltpu.VMEM((width, width), kind)
     image = pltpu.VMEM((width, width), jnp.float32)
-    short = pltpu.VMEM((width, width), jnp.bfloat16)
-    packets = pltpu.VMEM((2 * depth * 8, 128), jnp.float32)
-    out = pl.pallas_call(
+    packets = pltpu.VMEM((2 * depth, 8, 128), kind)
+    sharp = jax.ShapeDtypeStruct((width, width), jnp.float32)
+    coarse = jax.ShapeDtypeStruct((width, width), kind)
+    found = pl.pallas_call(
         functools.partial(whole_kernel, depth),
-        out_shape=jax.ShapeDtypeStruct(current.shape, jnp.float32),
-        in_specs=[pl.BlockSpec(memory_space=pltpu.VMEM)] * len(args),
-        out_specs=pl.BlockSpec(memory_space=pltpu.VMEM),
+        out_shape=(sharp, coarse, coarse, coarse),
+        in_specs=[pl.BlockSpec(memory_space=pl.ANY)] * 5 + [pl.BlockSpec(memory_space=pltpu.VMEM)] * (len(args) - 5),
+        out_specs=(pl.BlockSpec(memory_space=pltpu.VMEM),) * 4,
         scratch_shapes=built_shapes(1) + built_shapes(2) + built_shapes(2)
         + work_shapes(1, 1, width) + work_shapes(2, 2, depth)
-        + [short, short, pltpu.VMEM((4, width, 128), jnp.float32), image, image, packets, packets, packets, packets]
+        + [short, short, pltpu.VMEM((4, width, 128), jnp.float32), pltpu.VMEM((2 * depth * 8, 128), jnp.float32)]
+        + [packets] * 4
+        + [pltpu.VMEM((4, width, width), jnp.float32), image, image, short, short, pltpu.SemaphoreType.DMA((8,))]
         + [pltpu.SemaphoreType.DMA] * 6,
         compiler_params=pltpu.CompilerParams(vmem_limit_bytes=60 * 2**20, collective_id=0, has_side_effects=True),
         cost_estimate=pl.CostEstimate(flops=12 * 10**9, bytes_accessed=2**22, transcendentals=0),
     )(*args)
+    step = width // 4
+    flat = pl.BlockSpec((step, width), lambda i: (i, 0))
+    deep = pl.BlockSpec((4, step, width), lambda i: (0, i, 0))
+    out = pl.pallas_call(
+        final_kernel,
+        grid=(4,),
+        out_shape=jax.ShapeDtypeStruct(current.shape, jnp.float32),
+        in_specs=[deep, flat, flat, flat, flat],
+        out_specs=deep,
+        cost_estimate=pl.CostEstimate(flops=2 * 10**6, bytes_accessed=2**21, transcendentals=0),
+    )(current, *found)
     return out[:, None, None]
 
 

time: 59.9 us -> 51.1 us (0.85)
  local copies, waits for them, and re-layouts: 4.53 us -> 0 us
  Pallas kernels: 55.1 us -> 50.9 us
    unnamed x5 -> x0, local copies, waits for them, and re-layouts: 4.53 us -> none
    pallas_call x1 -> x2, Pallas kernels: 55.1 us -> 50.9 us  [the longest x1 47.4 us: on_device(): pl.pallas_call(functools.partial(whole_kernel, depth), out_shape=(sharp,...]
where the time goes in v3:
time: 51.1 us; the launch traced here: 50.9 us
  Pallas kernels  50.9 us (100%)
    pallas_call x1, Pallas kernels, on_device(): pl.pallas_call(functools.partial(whole_kernel, depth), out_shape=(sharp,...  47.4 us
    pallas_call x1, Pallas kernels, on_device(): pl.pallas_call(final_kernel, grid=(4,), out_shape=jax.ShapeDtypeStruct(cu...  3.52 us

profile of v3, /device:TPU:1, one launch (start us, length us, event | category | flops | bytes accessed | tf_op | source)
XLA Modules:
  0.0 50.9 jit_solution(7168601003544265299)
XLA Ops:
  0.0 47.4 %shard_map.136 = (f32[256,256]{1,0:T(8,128)}, bf16[256,256]{1,0:T(8,128)(2,1)}, bf16[256,256]{1,0:T(8,128)(2,1)}, bf16[256,256]{1,0:T(8,128)(2,1)}) custom-call(f32[4,256,256]{2,1,0:T(8,128)} %bitcast.7, f32[256,256]{1,0:T(8,128)} %bitcast.9, f32[256,256]{1,0:T(8,128)} %response_at.1, bf16[256,256]{1,0:T(8,128)(2,1)} %constant.12.clone.cosine_at, ...), custom_call_target="tpu_custom_call" | custom-call | flops 12000000000 | bytes 4194304 | tf_op jit(solution)/shard_map/pallas_call | solution.py:464
  47.4 3.5 %shard_map.137 = f32[4,256,256]{2,1,0:T(8,128)} custom-call(f32[4,256,256]{2,1,0:T(8,128)} %bitcast.8, f32[256,256]{1,0:T(8,128)} %get-tuple-element.9.data, bf16[256,256]{1,0:T(8,128)(2,1)} %get-tuple-element.10.res_z, bf16[256,256]{1,0:T(8,128)(2,1)} %get-tuple-element.11.res_x, bf16[256,256]{1,0:T(8,128)(2,1)} %get-tuple-element.12.res_y), custom_call_target="tpu_custom_call" | custom-call | flops 2000000 | bytes 2097152 | tf_op jit(solution)/shard_map/pallas_call | solution.py:481

commit v4 on v3

--- a/solution.py
+++ b/solution.py
@@ -206,7 +206,7 @@
     lax.fori_loop(0, rows // 8 // FIRST_STEP, first_layer, 0)
 
 
-def second_half(built, gather, emit, h_ref, c_ref, frames):
+def second_half(built, gather, emit, h_ref, c_ref, frames, between=None):
     w_mid, b_mid, w_last = built[2:5]
     images = h_ref.shape[0]
     row_blocks = h_ref.shape[1] - 2
@@ -237,7 +237,12 @@
             c_ref[img, a + 1 + k] = last[:, k * 128:(k + 1) * 128]
         return carry
 
-    lax.fori_loop(0, images * steps, mid_layer, 0)
+    if between is None:
+        lax.fori_loop(0, images * steps, mid_layer, 0)
+    else:
+        lax.fori_loop(0, 1, mid_layer, 0)
+        between()
+        lax.fori_loop(1, images * steps, mid_layer, 0)
 
     lane = lax.broadcasted_iota(jnp.int32, (row_blocks * 8, 128), 1)
     sub = lax.broadcasted_iota(jnp.int32, (row_blocks * 8, 128), 0) % 8
@@ -303,18 +308,23 @@
     rest = rest[13:]
     built = [rest[0:6], rest[6:12], rest[12:18]]
     z_work, xy_work = rest[18:21], rest[21:24]
-    z_own, z_other, turned, rows_f32, leaving, arrived, going, returned = rest[24:32]
-    states, measured, response, cosine, sines, loaded = rest[32:38]
-    z_send, z_recv, there_send, there_recv, back_send, back_recv = rest[38:]
+    z_own, z_other, turned, rows_f32 = rest[24:28]
+    there, back = rest[28:31], rest[31:34]
+    states, measured, response, cosine, sines, loaded = rest[34:40]
+    z_send, z_recv = rest[40:42]
+    there_sems, back_sems = rest[42:47], rest[47:52]
     kind = jnp.bfloat16
     devices = 2 * depth
     frame = lax.axis_index("frame")
     plane = lax.axis_index("plane")
-    me = frame * depth + plane
+    chips = devices // 2
+    chip = (frame * depth + plane) // 2
+    core = (frame * depth + plane) % 2
+    sibling = (frame, plane + 1 - 2 * core)
 
     def at(k):
-        other = me ^ k
-        return other, (other // depth, other % depth)
+        other = (chip ^ k) * 2 + core
+        return chip ^ k, (other // depth, other % depth)
 
     barrier = pltpu.get_barrier_semaphore()
 
@@ -327,7 +337,30 @@
         loads.append(pltpu.make_async_copy(source, target, loaded.at[4 + k]))
     for k in (2, 3, 1, 0, 4, 5, 6, 7):
         loads[k].start()
-    lax.fori_loop(1, devices, greet, 0, unroll=UNROLL)
+    pl.semaphore_signal(barrier, inc=1, device_id=sibling, device_id_type=MESH)
+    lax.fori_loop(1, chips, greet, 0, unroll=UNROLL)
+
+    def pack(buffer):
+        value = rows_f32[...].astype(kind).reshape(chips, 2, 8, 128)
+        buffer[0] = value[:, 0]
+        buffer[1] = value[:, 1]
+
+    def unpack_rows(buffer):
+        rows_f32[...] = buffer[...].astype(jnp.float32).reshape(devices * 8, 128)
+
+    def within_chip(buffers, sems):
+        source, mixed, _ = buffers
+        keep, send, recv, _, _ = sems
+        moves = [
+            pltpu.make_async_copy(source.at[core], mixed.at[:, core], keep),
+            pltpu.make_async_remote_copy(
+                src_ref=source.at[1 - core], dst_ref=mixed.at[:, core], send_sem=send, recv_sem=recv,
+                device_id=sibling, device_id_type=MESH,
+            ),
+        ]
+        for move in moves:
+            move.start()
+        return moves
 
     loads[2].wait()
     loads[3].wait()
@@ -337,47 +370,43 @@
         for p in range(2):
             for half in range(2):
                 rows_f32[pl.ds(which * 4 + p * 2 + half, devices, stride=8), :] = turned[which * 2 + half, pl.ds(p, devices, stride=2), :]
-    leaving[...] = rows_f32[...].reshape(devices, 8, 128).astype(kind)
+    pack(there[0])
     loads[1].wait()
     z_own[...] = states[1].astype(kind)
-    prepare(0, params, tables, built[0], 1)
-    pl.semaphore_wait(barrier, devices - 1)
-
-    def packet(ref, d):
-        return ref.at[d]
-
-    def exchange(source, target, send, recv):
-        pltpu.make_async_copy(packet(source, me), packet(target, me), recv).start()
+    pl.semaphore_wait(barrier, chips)
+
+    def between_chips(buffers, sems, moves):
+        _, mixed, target = buffers
+        _, _, _, send, recv = sems
+        for move in moves:
+            move.wait()
+        pltpu.make_async_copy(mixed.at[chip], target.at[chip], recv).start()
 
         def go(k, carry):
             other, coordinates = at(k)
             pltpu.make_async_remote_copy(
-                src_ref=packet(source, other),
-                dst_ref=packet(target, me),
-                send_sem=send,
-                recv_sem=recv,
-                device_id=coordinates,
-                device_id_type=MESH,
+                src_ref=mixed.at[other], dst_ref=target.at[chip], send_sem=send, recv_sem=recv,
+                device_id=coordinates, device_id_type=MESH,
             ).start()
             return carry
 
-        lax.fori_loop(1, devices, go, 0, unroll=UNROLL)
-
-    def all_sent(source, send):
-        some = source.at[pl.ds(0, devices - 1)]
-        pltpu.make_async_copy(some, some, send).wait()
-
-    def all_here(target, recv):
-        pltpu.make_async_copy(target, target, recv).wait()
-
+        lax.fori_loop(1, chips, go, 0, unroll=UNROLL)
+
+    def finish(buffers, sems):
+        _, mixed, target = buffers
+        pltpu.make_async_copy(target, target, sems[4]).wait()
+        some = mixed.at[pl.ds(0, chips - 1)]
+        pltpu.make_async_copy(some, some, sems[3]).wait()
+
+    there_moves = within_chip(there, there_sems)
     swap = pltpu.make_async_remote_copy(
         src_ref=z_own, dst_ref=z_other, send_sem=z_send, recv_sem=z_recv,
         device_id=(1 - frame, plane), device_id_type=MESH,
     )
     swap.start()
-    exchange(leaving, arrived, there_send, there_recv)
-
+    prepare(0, params, tables, built[0], 1)
     prepare(1, params, tables, built[1], 2)
+    between_chips(there, there_sems, there_moves)
     prepare(2, params, tables, built[2], 2)
     for k in (0, 4, 5, 6, 7):
         loads[k].wait()
@@ -386,9 +415,8 @@
     swap.wait()
     first_half([(lambda: z_own[...], lambda: z_other[...])], built[0], spread[...], *z_work, frames=1)
 
-    all_here(arrived, there_recv)
-    all_sent(leaving, there_send)
-    rows_f32[...] = arrived[...].astype(jnp.float32).reshape(devices * 8, 128)
+    finish(there, there_sems)
+    unpack_rows(there[2])
 
     def rows_of(which, p, f, half):
         return pl.ds(f * depth * 8 + which * 4 + p * 2 + half, depth, stride=8)
@@ -405,17 +433,15 @@
         pairs = [(functools.partial(plane_of, p, 0), functools.partial(plane_of, p, 1)) for p in range(2)]
         first_half(pairs, built[which + 1], spread[...], *xy_work, frames=2)
         second_half(built[which + 1], gather[...], emit, *xy_work[1:], frames=2)
-    going[...] = rows_f32[...].reshape(devices, 8, 128).astype(kind)
-    exchange(going, returned, back_send, back_recv)
+    pack(back[0])
+    back_moves = within_chip(back, back_sems)
 
     def emit_z(p, f, value):
         z_res[...] = value.astype(kind)
 
-    second_half(built[0], gather[...], emit_z, *z_work[1:], frames=1)
-    all_here(returned, back_recv)
-    all_sent(going, back_send)
-
-    rows_f32[...] = returned[...].astype(jnp.float32).reshape(devices * 8, 128)
+    second_half(built[0], gather[...], emit_z, *z_work[1:], frames=1, between=lambda: between_chips(back, back_sems, back_moves))
+    finish(back, back_sems)
+    unpack_rows(back[2])
 
     def unpack(which):
         for p in range(2):
@@ -458,7 +484,8 @@
     args += (jnp.transpose(kernel_in, (0, 1, 3, 2)), bias_in, kernel_mid, bias_mid, jnp.transpose(kernel_out, (1, 0, 2))) + constants(width)
     short = pltpu.VMEM((width, width), kind)
     image = pltpu.VMEM((width, width), jnp.float32)
-    packets = pltpu.VMEM((2 * depth, 8, 128), kind)
+    by_core = pltpu.VMEM((2, depth, 8, 128), kind)
+    by_chip = pltpu.VMEM((depth, 2, 8, 128), kind)
     sharp = jax.ShapeDtypeStruct((width, width), jnp.float32)
     coarse = jax.ShapeDtypeStruct((width, width), kind)
     found = pl.pallas_call(
@@ -469,18 +496,18 @@
         scratch_shapes=built_shapes(1) + built_shapes(2) + built_shapes(2)
         + work_shapes(1, 1, width) + work_shapes(2, 2, depth)
         + [short, short, pltpu.VMEM((4, width, 128), jnp.float32), pltpu.VMEM((2 * depth * 8, 128), jnp.float32)]
-        + [packets] * 4
+        + [by_core, by_chip, by_chip] * 2
         + [pltpu.VMEM((4, width, width), jnp.float32), image, image, short, short, pltpu.SemaphoreType.DMA((8,))]
-        + [pltpu.SemaphoreType.DMA] * 6,
+        + [pltpu.SemaphoreType.DMA] * 12,
         compiler_params=pltpu.CompilerParams(vmem_limit_bytes=60 * 2**20, collective_id=0, has_side_effects=True),
         cost_estimate=pl.CostEstimate(flops=12 * 10**9, bytes_accessed=2**22, transcendentals=0),
     )(*args)
-    step = width // 4
+    step = width // 2
     flat = pl.BlockSpec((step, width), lambda i: (i, 0))
     deep = pl.BlockSpec((4, step, width), lambda i: (0, i, 0))
     out = pl.pallas_call(
         final_kernel,
-        grid=(4,),
+        grid=(2,),
         out_shape=jax.ShapeDtypeStruct(current.shape, jnp.float32),
         in_specs=[deep, flat, flat, flat, flat],
         out_specs=deep,

time: 51.1 us -> 48.8 us (0.955)
  Pallas kernels: 50.9 us -> 48.7 us
    pallas_call x1, Pallas kernels: 3.52 us -> 2.3 us  [on_device(): pl.pallas_call(final_kernel, grid=(2,), out_shape=jax.ShapeDtypeStruct(cu...]
    pallas_call x1, Pallas kernels: 47.4 us -> 46.4 us  [on_device(): pl.pallas_call(functools.partial(whole_kernel, depth), out_shape=(sharp,...]
where the time goes in v4:
time: 48.8 us; the launch traced here: 48.7 us
  Pallas kernels  48.7 us (100%)
    pallas_call x1, Pallas kernels, on_device(): pl.pallas_call(functools.partial(whole_kernel, depth), out_shape=(sharp,...  46.4 us
    pallas_call x1, Pallas kernels, on_device(): pl.pallas_call(final_kernel, grid=(2,), out_shape=jax.ShapeDtypeStruct(cu...  2.3 us

profile of v4, /device:TPU:1, one launch (start us, length us, event | category | flops | bytes accessed | tf_op | source)
XLA Modules:
  0.0 48.7 jit_solution(3415858682279104021)
XLA Ops:
  0.0 46.4 %shard_map.136 = (f32[256,256]{1,0:T(8,128)}, bf16[256,256]{1,0:T(8,128)(2,1)}, bf16[256,256]{1,0:T(8,128)(2,1)}, bf16[256,256]{1,0:T(8,128)(2,1)}) custom-call(f32[4,256,256]{2,1,0:T(8,128)} %bitcast.7, f32[256,256]{1,0:T(8,128)} %bitcast.9, f32[256,256]{1,0:T(8,128)} %response_at.1, bf16[256,256]{1,0:T(8,128)(2,1)} %constant.12.clone.cosine_at, ...), custom_call_target="tpu_custom_call" | custom-call | flops 12000000000 | bytes 4194304 | tf_op jit(solution)/shard_map/pallas_call | solution.py:491
  46.4 2.3 %shard_map.137 = f32[4,256,256]{2,1,0:T(8,128)} custom-call(f32[4,256,256]{2,1,0:T(8,128)} %bitcast.8, f32[256,256]{1,0:T(8,128)} %get-tuple-element.9.data, bf16[256,256]{1,0:T(8,128)(2,1)} %get-tuple-element.10.res_z, bf16[256,256]{1,0:T(8,128)(2,1)} %get-tuple-element.11.res_x, bf16[256,256]{1,0:T(8,128)(2,1)} %get-tuple-element.12.res_y), custom_call_target="tpu_custom_call" | custom-call | flops 2000000 | bytes 2097152 | tf_op jit(solution)/shard_map/pallas_call | solution.py:508

commit v5 on v4

--- a/solution.py
+++ b/solution.py
@@ -206,7 +206,7 @@
     lax.fori_loop(0, rows // 8 // FIRST_STEP, first_layer, 0)
 
 
-def second_half(built, gather, emit, h_ref, c_ref, frames, between=None):
+def second_half(built, gather, emit, h_ref, c_ref, frames):
     w_mid, b_mid, w_last = built[2:5]
     images = h_ref.shape[0]
     row_blocks = h_ref.shape[1] - 2
@@ -237,12 +237,7 @@
             c_ref[img, a + 1 + k] = last[:, k * 128:(k + 1) * 128]
         return carry
 
-    if between is None:
-        lax.fori_loop(0, images * steps, mid_layer, 0)
-    else:
-        lax.fori_loop(0, 1, mid_layer, 0)
-        between()
-        lax.fori_loop(1, images * steps, mid_layer, 0)
+    lax.fori_loop(0, images * steps, mid_layer, 0)
 
     lane = lax.broadcasted_iota(jnp.int32, (row_blocks * 8, 128), 1)
     sub = lax.broadcasted_iota(jnp.int32, (row_blocks * 8, 128), 0) % 8
@@ -303,7 +298,7 @@
 
 
 def whole_kernel(depth, states_at, measured_at, response_at, cosine_at, sines_at, *rest):
-    params, tables, spread, gather = rest[:5], rest[5:7], rest[7], rest[8]
+    params, first_at, last_at, spread_at, gather_at = rest[:5], rest[5], rest[6], rest[7], rest[8]
     data, z_res, x_res, y_res = rest[9:13]
     rest = rest[13:]
     built = [rest[0:6], rest[6:12], rest[12:18]]
@@ -313,6 +308,8 @@
     states, measured, response, cosine, sines, loaded = rest[34:40]
     z_send, z_recv = rest[40:42]
     there_sems, back_sems = rest[42:47], rest[47:52]
+    first, spread, gather = rest[52:]
+    tables = first, last_at
     kind = jnp.bfloat16
     devices = 2 * depth
     frame = lax.axis_index("frame")
@@ -335,7 +332,9 @@
     loads = [pltpu.make_async_copy(states_at.at[k], states.at[k], loaded.at[k]) for k in range(4)]
     for k, (source, target) in enumerate(((measured_at, measured), (response_at, response), (cosine_at, cosine), (sines_at, sines))):
         loads.append(pltpu.make_async_copy(source, target, loaded.at[4 + k]))
-    for k in (2, 3, 1, 0, 4, 5, 6, 7):
+    for k, (source, target) in enumerate(((first_at, first), (spread_at, spread), (gather_at, gather))):
+        loads.append(pltpu.make_async_copy(source, target, loaded.at[8 + k]))
+    for k in (2, 3, 1, 8, 0, 4, 5, 6, 7, 9, 10):
         loads[k].start()
     pl.semaphore_signal(barrier, inc=1, device_id=sibling, device_id_type=MESH)
     lax.fori_loop(1, chips, greet, 0, unroll=UNROLL)
@@ -403,17 +402,16 @@
         src_ref=z_own, dst_ref=z_other, send_sem=z_send, recv_sem=z_recv,
         device_id=(1 - frame, plane), device_id_type=MESH,
     )
-    swap.start()
+    loads[8].wait()
     prepare(0, params, tables, built[0], 1)
     prepare(1, params, tables, built[1], 2)
     between_chips(there, there_sems, there_moves)
+    swap.start()
     prepare(2, params, tables, built[2], 2)
-    for k in (0, 4, 5, 6, 7):
+    for k in (0, 4, 5, 6, 7, 9, 10):
         loads[k].wait()
     source = (measured[...] + states[0]).astype(kind)
     data[...] = filtered(source, response[...], cosine[...], sines[...])
-    swap.wait()
-    first_half([(lambda: z_own[...], lambda: z_other[...])], built[0], spread[...], *z_work, frames=1)
 
     finish(there, there_sems)
     unpack_rows(there[2])
@@ -439,7 +437,10 @@
     def emit_z(p, f, value):
         z_res[...] = value.astype(kind)
 
-    second_half(built[0], gather[...], emit_z, *z_work[1:], frames=1, between=lambda: between_chips(back, back_sems, back_moves))
+    swap.wait()
+    first_half([(lambda: z_own[...], lambda: z_other[...])], built[0], spread[...], *z_work, frames=1)
+    between_chips(back, back_sems, back_moves)
+    second_half(built[0], gather[...], emit_z, *z_work[1:], frames=1)
     finish(back, back_sems)
     unpack_rows(back[2])
 
@@ -491,14 +492,15 @@
     found = pl.pallas_call(
         functools.partial(whole_kernel, depth),
         out_shape=(sharp, coarse, coarse, coarse),
-        in_specs=[pl.BlockSpec(memory_space=pl.ANY)] * 5 + [pl.BlockSpec(memory_space=pltpu.VMEM)] * (len(args) - 5),
+        in_specs=[pl.BlockSpec(memory_space=pltpu.VMEM if 5 <= k < 10 or k == 11 else pl.ANY) for k in range(len(args))],
         out_specs=(pl.BlockSpec(memory_space=pltpu.VMEM),) * 4,
         scratch_shapes=built_shapes(1) + built_shapes(2) + built_shapes(2)
         + work_shapes(1, 1, width) + work_shapes(2, 2, depth)
         + [short, short, pltpu.VMEM((4, width, 128), jnp.float32), pltpu.VMEM((2 * depth * 8, 128), jnp.float32)]
         + [by_core, by_chip, by_chip] * 2
-        + [pltpu.VMEM((4, width, width), jnp.float32), image, image, short, short, pltpu.SemaphoreType.DMA((8,))]
-        + [pltpu.SemaphoreType.DMA] * 12,
+        + [pltpu.VMEM((4, width, width), jnp.float32), image, image, short, short, pltpu.SemaphoreType.DMA((11,))]
+        + [pltpu.SemaphoreType.DMA] * 12
+        + [pltpu.VMEM(table.shape, kind) for table in (args[10], args[12], args[13])],
         compiler_params=pltpu.CompilerParams(vmem_limit_bytes=60 * 2**20, collective_id=0, has_side_effects=True),
         cost_estimate=pl.CostEstimate(flops=12 * 10**9, bytes_accessed=2**22, transcendentals=0),
     )(*args)

time: 48.8 us -> 48.8 us (level); the launches traced: 48.7 us -> 48.1 us
  Pallas kernels: 48.7 us -> 48 us
    pallas_call x1, Pallas kernels: 46.4 us -> 45.7 us  [on_device(): pl.pallas_call(functools.partial(whole_kernel, depth), out_shape=(sharp,...]
where the time goes in v5:
time: 48.8 us; the launch traced here: 48.1 us
  Pallas kernels  48 us (98%)
    pallas_call x1, Pallas kernels, on_device(): pl.pallas_call(functools.partial(whole_kernel, depth), out_shape=(sharp,...  45.7 us
    pallas_call x1, Pallas kernels, on_device(): pl.pallas_call(final_kernel, grid=(2,), out_shape=jax.ShapeDtypeStruct(cu...  2.3 us

profile of v5, /device:TPU:1, one launch (start us, length us, event | category | flops | bytes accessed | tf_op | source)
XLA Modules:
  0.0 48.1 jit_solution(13706704601896669439)
XLA Ops:
  0.0 45.7 %shard_map.136 = (f32[256,256]{1,0:T(8,128)}, bf16[256,256]{1,0:T(8,128)(2,1)}, bf16[256,256]{1,0:T(8,128)(2,1)}, bf16[256,256]{1,0:T(8,128)(2,1)}) custom-call(f32[4,256,256]{2,1,0:T(8,128)} %bitcast.7, f32[256,256]{1,0:T(8,128)} %bitcast.9, f32[256,256]{1,0:T(8,128)} %response_at.1, bf16[256,256]{1,0:T(8,128)(2,1)} %constant.12.clone.cosine_at, ...), custom_call_target="tpu_custom_call" | custom-call | flops 12000000000 | bytes 4194304 | tf_op jit(solution)/shard_map/pallas_call | solution.py:492
  45.7 2.3 %shard_map.137 = f32[4,256,256]{2,1,0:T(8,128)} custom-call(f32[4,256,256]{2,1,0:T(8,128)} %bitcast.8, f32[256,256]{1,0:T(8,128)} %get-tuple-element.9.data, bf16[256,256]{1,0:T(8,128)(2,1)} %get-tuple-element.10.res_z, bf16[256,256]{1,0:T(8,128)(2,1)} %get-tuple-element.11.res_x, bf16[256,256]{1,0:T(8,128)(2,1)} %get-tuple-element.12.res_y), custom_call_target="tpu_custom_call" | custom-call | flops 2000000 | bytes 2097152 | tf_op jit(solution)/shard_map/pallas_call | solution.py:510

commit v6 on v4

--- a/solution.py
+++ b/solution.py
@@ -212,17 +212,18 @@
     row_blocks = h_ref.shape[1] - 2
     rows = row_blocks * 4
     kind = jnp.bfloat16
-    n = MID_STEP * 128
+    together = min(2, images)
+    n = together * MID_STEP * 128
     right = (lax.broadcasted_iota(jnp.int32, (n, 256), 1) // 32) % 2 == 1
     right_half = right[:, :128]
     low = lax.broadcasted_iota(jnp.int32, (n, 128), 1) >= 64
     steps = row_blocks // MID_STEP
 
     def mid_layer(at, carry):
-        img, a = at // steps, (at % steps) * MID_STEP
+        img, a = at // steps * together, (at % steps) * MID_STEP
 
         def part(down, shift, lanes):
-            return h_ref[img, pl.ds(a + 1 + down, MID_STEP), 16 + shift:144 + shift, 0:lanes].reshape(n, lanes)
+            return h_ref[pl.ds(img, together), pl.ds(a + 1 + down, MID_STEP), 16 + shift:144 + shift, 0:lanes].reshape(n, lanes)
 
         here = part(0, 0, 256)
         side = jnp.where(right, part(0, -16, 256), part(0, 16, 256))
@@ -233,16 +234,18 @@
         made = mm(jnp.concatenate([here, side, across, corner], 1), w_mid[...])
         hidden = jnp.maximum(made + b_mid[0:1, :], 0.0).astype(kind)
         last = mm(w_last[...], hidden, ((1,), (1,)))
-        for k in range(MID_STEP):
-            c_ref[img, a + 1 + k] = last[:, k * 128:(k + 1) * 128]
+        for i in range(together):
+            for k in range(MID_STEP):
+                column = (i * MID_STEP + k) * 128
+                c_ref[img + i, a + 1 + k] = last[:, column:column + 128]
         return carry
 
     if between is None:
-        lax.fori_loop(0, images * steps, mid_layer, 0)
+        lax.fori_loop(0, images // together * steps, mid_layer, 0)
     else:
         lax.fori_loop(0, 1, mid_layer, 0)
         between()
-        lax.fori_loop(1, images * steps, mid_layer, 0)
+        lax.fori_loop(1, images // together * steps, mid_layer, 0)
 
     lane = lax.broadcasted_iota(jnp.int32, (row_blocks * 8, 128), 1)
     sub = lax.broadcasted_iota(jnp.int32, (row_blocks * 8, 128), 0) % 8

time: 48.8 us -> 47.9 us (0.982)
  Pallas kernels: 48.7 us -> 47.7 us
    pallas_call x1, Pallas kernels: 46.4 us -> 45.4 us  [on_device(): pl.pallas_call(functools.partial(whole_kernel, depth), out_shape=(sharp,...]
where the time goes in v6:
time: 47.9 us; the launch traced here: 47.7 us
  Pallas kernels  47.7 us (100%)
    pallas_call x1, Pallas kernels, on_device(): pl.pallas_call(functools.partial(whole_kernel, depth), out_shape=(sharp,...  45.4 us
    pallas_call x1, Pallas kernels, on_device(): pl.pallas_call(final_kernel, grid=(2,), out_shape=jax.ShapeDtypeStruct(cu...  2.3 us

profile of v6, /device:TPU:1, one launch (start us, length us, event | category | flops | bytes accessed | tf_op | source)
XLA Modules:
  0.0 47.7 jit_solution(14603228533337806432)
XLA Ops:
  0.0 45.4 %shard_map.136 = (f32[256,256]{1,0:T(8,128)}, bf16[256,256]{1,0:T(8,128)(2,1)}, bf16[256,256]{1,0:T(8,128)(2,1)}, bf16[256,256]{1,0:T(8,128)(2,1)}) custom-call(f32[4,256,256]{2,1,0:T(8,128)} %bitcast.7, f32[256,256]{1,0:T(8,128)} %bitcast.9, f32[256,256]{1,0:T(8,128)} %response_at.1, bf16[256,256]{1,0:T(8,128)(2,1)} %constant.12.clone.cosine_at, ...), custom_call_target="tpu_custom_call" | custom-call | flops 12000000000 | bytes 4194304 | tf_op jit(solution)/shard_map/pallas_call | solution.py:494
  45.4 2.3 %shard_map.137 = f32[4,256,256]{2,1,0:T(8,128)} custom-call(f32[4,256,256]{2,1,0:T(8,128)} %bitcast.8, f32[256,256]{1,0:T(8,128)} %get-tuple-element.9.data, bf16[256,256]{1,0:T(8,128)(2,1)} %get-tuple-element.10.res_z, bf16[256,256]{1,0:T(8,128)(2,1)} %get-tuple-element.11.res_x, bf16[256,256]{1,0:T(8,128)(2,1)} %get-tuple-element.12.res_y), custom_call_target="tpu_custom_call" | custom-call | flops 2000000 | bytes 2097152 | tf_op jit(solution)/shard_map/pallas_call | solution.py:511
